TPU v7x, 256 devices: a whole 4x4x8 slice. The times are simulated.
256 devices in a mesh: ctx: 32 (over z_lo, x, core), tp: 8 (over y, z_hi).
Axes of the slice: x: 4, y: 4, z: 8 (z_hi: 2, z_lo: 4; z = z_hi * 4 + z_lo), core: 2. Of those that a mesh axis runs over, the one named last changes fastest.
Arguments:
- query_heads: bfloat16 [8192, 4096], P('ctx', 'tp'), may hold values from -8 to 8
- key_heads: bfloat16 [8192, 4096], P('ctx', 'tp'), may hold values from -8 to 8
- value_heads: bfloat16 [8192, 4096], P('ctx', 'tp'), may hold values from -6 to 6
- grad_heads: bfloat16 [8192, 4096], P('ctx', 'tp'), may hold values from -6 to 6
- counts: int32 [32], replicated, may hold values from 1 to 256, as said below
Outputs:
- attended: bfloat16 [8192, 4096], P('ctx', 'tp')
- grad_query: bfloat16 [8192, 4096], P('ctx', 'tp')
- grad_key: bfloat16 [8192, 4096], P('ctx', 'tp')
- grad_value: bfloat16 [8192, 4096], P('ctx', 'tp')
Inputs may be any that keep to these rules, and one draw needn't show every extreme that they name: counts[s] is the number of kept slots of shard s, which are its first ones; some shard is full in every draw.
All inputs are finite; a program needn't handle non-finite values.
Results may differ from a plain program's by a relative error of at most 0.03.
Values may be sent and summed in bfloat16 or wider, within the bound.
A program may use at most 192 MiB of HBM per device.

v0:
```python
import jax
import jax.numpy as jnp
from jax import lax
from jax.sharding import PartitionSpec as P

HD = 128
QB = 32
KB = 512


far_away = 1073741824
very_low = -1e30


def effective(positions, counts, group_rows, fill_value):
    slot_index = lax.iota(jnp.int32, positions.shape[0])
    kept_limit = jnp.repeat(counts, group_rows, total_repeat_length=positions.shape[0])
    return jnp.where(slot_index % group_rows < kept_limit, positions, fill_value)


def compact_rows(counts, group_rows, total_rows):
    group_ends = jnp.cumsum(counts)
    starts = group_ends - counts
    slot_index = lax.iota(jnp.int32, total_rows)
    group_of = jnp.sum((group_ends[None, :] <= slot_index[:, None]).astype(jnp.int32), axis=1)
    group_of = jnp.minimum(group_of, counts.shape[0] - 1)
    chosen = lax.iota(jnp.int32, counts.shape[0])[None, :] == group_of[:, None]
    group_start = jnp.sum(jnp.where(chosen, starts[None, :], 0), axis=1)
    live_slot = slot_index < group_ends[-1]
    source = jnp.where(live_slot, group_of * group_rows + slot_index - group_start, 0)
    return (source, live_slot)


def query_side(query_rows, grad_rows, query_pos, live_rows, key_rows, value_rows, key_pos):
    row_total, head_count, head_dim = query_rows.shape
    softmax_scale = head_dim ** (-0.5)
    outputs = (
        jnp.zeros((row_total, head_count, head_dim), jnp.bfloat16),
        jnp.zeros((row_total, head_count, head_dim), jnp.bfloat16),
        jnp.zeros((row_total, head_count), jnp.float32),
        jnp.zeros((row_total, head_count), jnp.float32),
    )

    def query_per_block(block_index, carried):
        row_start = block_index * QB
        query_block = lax.dynamic_slice_in_dim(query_rows, row_start, QB, 0)
        grad_block = lax.dynamic_slice_in_dim(grad_rows, row_start, QB, 0)
        pos_block = lax.dynamic_slice_in_dim(query_pos, row_start, QB, 0)
        reach_count = jnp.sum((key_pos <= jnp.max(pos_block)).astype(jnp.int32))
        key_steps = (reach_count + KB - 1) // KB

        def tiles(key_index):
            key_start = key_index * KB
            key_block = lax.dynamic_slice_in_dim(key_rows, key_start, KB, 0)
            value_block = lax.dynamic_slice_in_dim(value_rows, key_start, KB, 0)
            key_pos_block = lax.dynamic_slice_in_dim(key_pos, key_start, KB, 0)
            scores = (
                jnp.einsum(
                    "qhd,khd->hqk", query_block, key_block, preferred_element_type=jnp.float32
                )
                * softmax_scale
            )
            allowed = (key_pos_block[None, :] <= pos_block[:, None])[None]
            return (key_start, key_block, value_block, scores, allowed)

        def forward_step(key_index, loop_state):
            row_best, weight_sum, accumulated = loop_state
            key_start, key_block, value_block, scores, allowed = tiles(key_index)
            new_best = jnp.maximum(row_best, jnp.max(jnp.where(allowed, scores, very_low), axis=-1))
            weights = jnp.where(allowed, jnp.exp(scores - new_best[..., None]), 0.0)
            factor = jnp.exp(row_best - new_best)
            weight_sum = weight_sum * factor + jnp.sum(weights, axis=-1)
            accumulated = accumulated * jnp.transpose(factor)[:, :, None] + jnp.einsum(
                "hqk,khd->qhd",
                weights.astype(jnp.bfloat16),
                value_block,
                preferred_element_type=jnp.float32,
            )
            return (new_best, weight_sum, accumulated)

        start_state = (
            jnp.full((head_count, QB), very_low, jnp.float32),
            jnp.zeros((head_count, QB), jnp.float32),
            jnp.zeros((QB, head_count, head_dim), jnp.float32),
        )
        row_best, weight_sum, accumulated = lax.fori_loop(0, key_steps, forward_step, start_state)
        live_block = pos_block >= 0
        safe_sum = jnp.where(live_block[None, :], weight_sum, 1.0)
        out_block = (accumulated / jnp.transpose(safe_sum)[:, :, None]).astype(jnp.bfloat16)
        log_sum = jnp.where(live_block[None, :], row_best + jnp.log(safe_sum), 0.0)
        row_delta = jnp.sum(out_block.astype(jnp.float32) * grad_block.astype(jnp.float32), axis=-1)
        delta_rows = jnp.transpose(row_delta)

        def backward_step(key_index, loop_state):
            key_start, key_block, value_block, scores, allowed = tiles(key_index)
            soft_probs = jnp.where(allowed, jnp.exp(scores - log_sum[..., None]), 0.0)
            grad_probs = jnp.einsum(
                "qhd,khd->hqk", grad_block, value_block, preferred_element_type=jnp.float32
            )
            grad_scores = (soft_probs * (grad_probs - delta_rows[..., None])).astype(jnp.bfloat16)
            query_grad = loop_state[0] + jnp.einsum(
                "hqk,khd->qhd", grad_scores, key_block, preferred_element_type=jnp.float32
            )
            return (query_grad,)

        back_state = (jnp.zeros((QB, head_count, head_dim), jnp.float32),)
        back_state = lax.fori_loop(0, key_steps, backward_step, back_state)
        query_grad = (back_state[0] * softmax_scale).astype(jnp.bfloat16)
        updated = (
            lax.dynamic_update_slice_in_dim(carried[0], out_block, row_start, 0),
            lax.dynamic_update_slice_in_dim(carried[1], query_grad, row_start, 0),
            lax.dynamic_update_slice_in_dim(carried[2], jnp.transpose(log_sum), row_start, 0),
            lax.dynamic_update_slice_in_dim(carried[3], row_delta, row_start, 0),
        )
        return updated

    block_count = (live_rows + QB - 1) // QB
    return lax.fori_loop(0, block_count, query_per_block, outputs)


def key_side(
    key_rows,
    value_rows,
    key_pos,
    live_rows,
    query_rows,
    grad_rows,
    log_sums,
    deltas,
    query_pos,
    query_live,
):
    row_total, head_count, head_dim = key_rows.shape
    softmax_scale = head_dim ** (-0.5)
    outputs = (
        jnp.zeros((row_total, head_count, head_dim), jnp.float32),
        jnp.zeros((row_total, head_count, head_dim), jnp.float32),
    )
    query_end = (query_live + KB - 1) // KB

    def key_per_block(block_index, carried):
        row_start = block_index * QB
        key_block = lax.dynamic_slice_in_dim(key_rows, row_start, QB, 0)
        value_block = lax.dynamic_slice_in_dim(value_rows, row_start, QB, 0)
        pos_block = lax.dynamic_slice_in_dim(key_pos, row_start, QB, 0)
        skipped = jnp.sum(((query_pos >= 0) & (query_pos < pos_block[0])).astype(jnp.int32))

        def step(query_index, loop_state):
            query_start = query_index * KB
            query_block = lax.dynamic_slice_in_dim(query_rows, query_start, KB, 0)
            grad_block = lax.dynamic_slice_in_dim(grad_rows, query_start, KB, 0)
            lse_block = jnp.transpose(lax.dynamic_slice_in_dim(log_sums, query_start, KB, 0))
            delta_block = jnp.transpose(lax.dynamic_slice_in_dim(deltas, query_start, KB, 0))
            query_pos_block = lax.dynamic_slice_in_dim(query_pos, query_start, KB, 0)
            scores = (
                jnp.einsum(
                    "qhd,khd->hqk", query_block, key_block, preferred_element_type=jnp.float32
                )
                * softmax_scale
            )
            allowed = (pos_block[None, :] <= query_pos_block[:, None])[None]
            soft_probs = jnp.where(allowed, jnp.exp(scores - lse_block[..., None]), 0.0)
            value_grad = loop_state[1] + jnp.einsum(
                "hqk,qhd->khd",
                soft_probs.astype(jnp.bfloat16),
                grad_block,
                preferred_element_type=jnp.float32,
            )
            grad_probs = jnp.einsum(
                "qhd,khd->hqk", grad_block, value_block, preferred_element_type=jnp.float32
            )
            grad_scores = (soft_probs * (grad_probs - delta_block[..., None])).astype(jnp.bfloat16)
            key_grad = loop_state[0] + jnp.einsum(
                "hqk,qhd->khd", grad_scores, query_block, preferred_element_type=jnp.float32
            )
            return (key_grad, value_grad)

        start_state = (
            jnp.zeros((QB, head_count, head_dim), jnp.float32),
            jnp.zeros((QB, head_count, head_dim), jnp.float32),
        )
        key_grad, value_grad = lax.fori_loop(skipped // KB, query_end, step, start_state)
        return (
            lax.dynamic_update_slice_in_dim(carried[0], key_grad, row_start, 0),
            lax.dynamic_update_slice_in_dim(carried[1], value_grad, row_start, 0),
        )

    block_count = (live_rows + QB - 1) // QB
    return lax.fori_loop(0, block_count, key_per_block, outputs)


def on_device(query_heads, key_heads, value_heads, grad_heads, counts):
    slot_cap, row_width = query_heads.shape
    head_count = row_width // HD
    softmax_scale = HD ** (-0.5)
    ctx_size = lax.axis_size("ctx")
    shard_index = lax.axis_index("ctx")
    slot_total = slot_cap * ctx_size
    all_pos = lax.iota(jnp.int32, slot_total)
    key_eff = effective(all_pos, counts, slot_cap, far_away)
    query_eff = effective(all_pos, counts, slot_cap, -1)
    own_live = counts[shard_index]
    own_query_pos = lax.dynamic_slice_in_dim(query_eff, shard_index * slot_cap, slot_cap, 0)
    own_key_pos = lax.dynamic_slice_in_dim(key_eff, shard_index * slot_cap, slot_cap, 0)
    keys_all, values_all = (
        lax.all_gather(key_heads, "ctx", axis=0, tiled=True),
        lax.all_gather(value_heads, "ctx", axis=0, tiled=True),
    )
    padded = -(-slot_total // KB) * KB
    source, live_slot = compact_rows(counts, slot_cap, padded)
    key_comp = keys_all[source].reshape(padded, head_count, HD)
    value_comp = values_all[source].reshape(padded, head_count, HD)
    key_pos_comp = jnp.where(live_slot, key_eff[source], far_away)
    total_live = jnp.sum(counts)
    results = query_side(
        query_heads.reshape(slot_cap, head_count, HD),
        grad_heads.reshape(slot_cap, head_count, HD),
        own_query_pos,
        own_live,
        key_comp,
        value_comp,
        key_pos_comp,
    )
    attended = results[0].reshape(slot_cap, row_width)
    grad_query = results[1].reshape(slot_cap, row_width)
    stat_lse = results[2]
    stat_delta = results[3]
    queries_all, grads_all = (
        lax.all_gather(query_heads, "ctx", axis=0, tiled=True),
        lax.all_gather(grad_heads, "ctx", axis=0, tiled=True),
    )
    lse_all, delta_all = (
        lax.all_gather(stat_lse, "ctx", axis=0, tiled=True),
        lax.all_gather(stat_delta, "ctx", axis=0, tiled=True),
    )
    query_comp = queries_all[source].reshape(padded, head_count, HD)
    grad_comp = grads_all[source].reshape(padded, head_count, HD)
    query_pos_comp = jnp.where(live_slot, query_eff[source], -1)
    key_grad, value_grad = key_side(
        key_heads.reshape(slot_cap, head_count, HD),
        value_heads.reshape(slot_cap, head_count, HD),
        own_key_pos,
        own_live,
        query_comp,
        grad_comp,
        lse_all[source],
        delta_all[source],
        query_pos_comp,
        total_live,
    )
    grad_key = (key_grad * softmax_scale).reshape(slot_cap, row_width).astype(jnp.bfloat16)
    grad_value = value_grad.reshape(slot_cap, row_width).astype(jnp.bfloat16)
    return (attended, grad_query, grad_key, grad_value)


def solution(mesh):
    return jax.shard_map(
        on_device,
        mesh=mesh,
        in_specs=(P("ctx", "tp"), P("ctx", "tp"), P("ctx", "tp"), P("ctx", "tp"), P()),
        out_specs=(P("ctx", "tp"), P("ctx", "tp"), P("ctx", "tp"), P("ctx", "tp")),
        check_vma=False,
    )
```

profile of v0, /device:TPU:1, one launch (start us, length us, event | category | flops | bytes accessed | tf_op | source)
XLA Modules:
  0.0 1299.8 jit_solution(719536302280874945)
XLA Ops:
  20.7 20.8 %iota_select_fusion = (s32[8192]{0:T(1024)S(1)}, pred[8192]{0:T(1024)(128)(4,1)S(1)}) fusion(pred[8192]{0:T(1024)(128)(4,1)} %constant.452, pred[8192]{0:T(1024)(128)(4,1)} %constant.453, pred[8192]{0:T(1024)(128)(4,1)} %constant.454, pred[8192]{0:T(1024)(128)(4,1)} %constant.455, pred[8192]{0:T(1024)(128)(4,1)} %constant.456, ...), kind=kLoop, calls=%fused_computation.107 | loop fusion | flops 319488 | bytes 295040 | tf_op jit(solution)/shard_map/jit(_where)/select_n | solution.py:18
  41.5 45.5 %gather_fusion = s32[8192]{0:T(1024)S(1)} fusion(s32[8192]{0:T(1024)S(1)} %get-tuple-element.953, s32[8192]{0:T(1024)S(1)} %broadcast_clamp_fusion), kind=kCustom, calls=%fused_computation | custom fusion | bytes 98304 | tf_op jit(solution)/shard_map/gather | solution.py:213
  87.1 45.5 %gather_fusion.3 = s32[8192]{0:T(1024)S(1)} fusion(s32[8192]{0:T(1024)S(1)} %iota_select_fusion.1, s32[8192]{0:T(1024)S(1)} %broadcast_clamp_fusion), kind=kCustom, calls=%fused_computation.3 | custom fusion | bytes 98304 | tf_op jit(solution)/shard_map/gather | solution.py:238
  138.8 38.5 %gather_fusion.1 = bf16[8192,512]{1,0:T(8,128)(2,1)} fusion(bf16[8192,512]{1,0:T(8,128)(2,1)} %all-gather.5.cloned.1.call-done, s32[8192]{0:T(1024)S(1)} %broadcast_clamp_fusion), kind=kCustom, calls=%fused_computation.1 | custom fusion | bytes 16809984 | tf_op jit(solution)/shard_map/gather | solution.py:211
  177.3 38.5 %gather_fusion.2 = bf16[8192,512]{1,0:T(8,128)(2,1)} fusion(bf16[8192,512]{1,0:T(8,128)(2,1)} %all-gather.7.cloned.1.call-done, s32[8192]{0:T(1024)S(1)} %broadcast_clamp_fusion), kind=kCustom, calls=%fused_computation.2 | custom fusion | bytes 16809984 | tf_op jit(solution)/shard_map/gather | solution.py:212
  215.8 11.4 copy_bitcast_fusion.2
  227.4 77.4 %while.143 = (s32[]{:T(128)}, bf16[256,4,128]{2,1,0:T(4,128)(2,1)S(1)}, bf16[256,4,128]{2,1,0:T(4,128)(2,1)S(1)}, f32[256,4]{0,1:T(4,128)S(1)}, f32[256,4]{1,0:T...) while((s32[]{:T(128)}, ...), condition=%wide.region_13.15_spmd, body=%wide.region_3.14_spmd.sunk | while | flops 85107424 | bytes 5077831 | solution.py:118
  230.0 3.2 while.146
  239.6 3.2 while.146
  249.3 3.2 while.146
  259.0 3.2 while.146
  262.6 3.2 while.147
  268.7 3.2 while.146
  278.3 3.2 while.146
  288.0 3.2 while.146
  297.7 3.2 while.146
  304.9 418.9 %all_gather.21 = f32[8192,4]{1,0:T(8,128)} all-gather(f32[256,4]{1,0:T(8,128)S(1)} %copy.97), channel_id=1, replica_groups=mesh['ctx'=32,'tp'=8] {'ctx'}, dimensions={0}, use_global_device_ids=true | all-gather | bytes 135168 | tf_op jit(solution)/shard_map/all_gather | solution.py:233
  723.8 30.1 %gather_fusion.5 = f32[8192,4]{1,0:T(8,128)} fusion(f32[8192,4]{1,0:T(8,128)} %all_gather.21, s32[8192]{0:T(1024)S(1)} %broadcast_clamp_fusion), kind=kCustom, calls=%fused_computation.5 | custom fusion | bytes 294912 | tf_op jit(solution)/shard_map/gather | solution.py:246
  756.7 53.4 %all_gather.23 = f32[8192,4]{1,0:T(8,128)} all-gather(f32[256,4]{1,0:T(8,128)S(1)} %get-tuple-element.649), channel_id=1, replica_groups=mesh['ctx'=32,'tp'=8] {'ctx'}, dimensions={0}, use_global_device_ids=true | all-gather | bytes 135168 | tf_op jit(solution)/shard_map/all_gather | solution.py:234
  810.1 30.1 %gather_fusion.7 = f32[8192,4]{1,0:T(8,128)} fusion(f32[8192,4]{1,0:T(8,128)} %all_gather.23, s32[8192]{0:T(1024)S(1)} %broadcast_clamp_fusion), kind=kCustom, calls=%fused_computation.7 | custom fusion | bytes 294912 | tf_op jit(solution)/shard_map/gather | solution.py:247
  843.0 38.4 %gather_fusion.4 = bf16[8192,512]{1,0:T(8,128)(2,1)} fusion(bf16[8192,512]{1,0:T(8,128)(2,1)} %all-gather.9.cloned.1.call-done, s32[8192]{0:T(1024)S(1)} %broadcast_clamp_fusion), kind=kCustom, calls=%fused_computation.4 | custom fusion | bytes 16809984 | tf_op jit(solution)/shard_map/gather | solution.py:236
  881.4 38.4 %gather_fusion.6 = bf16[8192,512]{1,0:T(8,128)(2,1)} fusion(bf16[8192,512]{1,0:T(8,128)(2,1)} %all-gather.11.cloned.1.call-done, s32[8192]{0:T(1024)S(1)} %broadcast_clamp_fusion), kind=kCustom, calls=%fused_computation.6 | custom fusion | bytes 16809984 | tf_op jit(solution)/shard_map/gather | solution.py:237
  919.8 11.4 copy_bitcast_fusion
  931.3 359.0 %while.145 = (s32[]{:T(128)}, f32[256,4,128]{2,0,1:T(8,128)S(1)}, bf16[256,4,128]{2,0,1:T(8,128)(2,1)S(1)}, s32[]{:T(128)}, s32[8192]{0:T(1024)S(1)}, /*index=5*...) while((s32[]{:T(128)}, f32[256,4,128]{2,0,1:T(8,128)S(1)}, ...), condition=%wide.region_19.21_spmd, body=%wide.region_15.20_spmd.sunk | while | flops 67657744 | bytes 3858588 | solution.py:189
  936.2 39.9 %while.148 = (s32[]{:T(128)}, f32[32,4,128]{2,0,1:T(8,128)S(1)}, f32[32,4,128]{2,0,1:T(8,128)S(1)}, s32[]{:T(128)}, bf16[8192,4,128]{2,0,1:T(8,128)(2,1)}, /*ind...) while((s32[]{:T(128)}, f32[32,4,128]{2,0,1:T(8,128)S(1)}, ...), condition=%wide.region_18.19_spmd, body=%wide.region_17.18_spmd.sunk | while | flops 67616768 | bytes 3300691 | solution.py:182
  981.1 39.9 %while.148 = (s32[]{:T(128)}, f32[32,4,128]{2,0,1:T(8,128)S(1)}, f32[32,4,128]{2,0,1:T(8,128)S(1)}, s32[]{:T(128)}, bf16[8192,4,128]{2,0,1:T(8,128)(2,1)}, /*ind...) while((s32[]{:T(128)}, f32[32,4,128]{2,0,1:T(8,128)S(1)}, ...), condition=%wide.region_18.19_spmd, body=%wide.region_17.18_spmd.sunk | while | flops 67616768 | bytes 3300691 | solution.py:182
  1026.0 39.9 %while.148 = (s32[]{:T(128)}, f32[32,4,128]{2,0,1:T(8,128)S(1)}, f32[32,4,128]{2,0,1:T(8,128)S(1)}, s32[]{:T(128)}, bf16[8192,4,128]{2,0,1:T(8,128)(2,1)}, /*ind...) while((s32[]{:T(128)}, f32[32,4,128]{2,0,1:T(8,128)S(1)}, ...), condition=%wide.region_18.19_spmd, body=%wide.region_17.18_spmd.sunk | while | flops 67616768 | bytes 3300691 | solution.py:182
  1070.9 39.9 %while.148 = (s32[]{:T(128)}, f32[32,4,128]{2,0,1:T(8,128)S(1)}, f32[32,4,128]{2,0,1:T(8,128)S(1)}, s32[]{:T(128)}, bf16[8192,4,128]{2,0,1:T(8,128)(2,1)}, /*ind...) while((s32[]{:T(128)}, f32[32,4,128]{2,0,1:T(8,128)S(1)}, ...), condition=%wide.region_18.19_spmd, body=%wide.region_17.18_spmd.sunk | while | flops 67616768 | bytes 3300691 | solution.py:182
  1115.7 39.9 %while.148 = (s32[]{:T(128)}, f32[32,4,128]{2,0,1:T(8,128)S(1)}, f32[32,4,128]{2,0,1:T(8,128)S(1)}, s32[]{:T(128)}, bf16[8192,4,128]{2,0,1:T(8,128)(2,1)}, /*ind...) while((s32[]{:T(128)}, f32[32,4,128]{2,0,1:T(8,128)S(1)}, ...), condition=%wide.region_18.19_spmd, body=%wide.region_17.18_spmd.sunk | while | flops 67616768 | bytes 3300691 | solution.py:182
  1160.6 39.9 %while.148 = (s32[]{:T(128)}, f32[32,4,128]{2,0,1:T(8,128)S(1)}, f32[32,4,128]{2,0,1:T(8,128)S(1)}, s32[]{:T(128)}, bf16[8192,4,128]{2,0,1:T(8,128)(2,1)}, /*ind...) while((s32[]{:T(128)}, f32[32,4,128]{2,0,1:T(8,128)S(1)}, ...), condition=%wide.region_18.19_spmd, body=%wide.region_17.18_spmd.sunk | while | flops 67616768 | bytes 3300691 | solution.py:182
  1205.5 39.9 %while.148 = (s32[]{:T(128)}, f32[32,4,128]{2,0,1:T(8,128)S(1)}, f32[32,4,128]{2,0,1:T(8,128)S(1)}, s32[]{:T(128)}, bf16[8192,4,128]{2,0,1:T(8,128)(2,1)}, /*ind...) while((s32[]{:T(128)}, f32[32,4,128]{2,0,1:T(8,128)S(1)}, ...), condition=%wide.region_18.19_spmd, body=%wide.region_17.18_spmd.sunk | while | flops 67616768 | bytes 3300691 | solution.py:182
  1250.4 39.9 %while.148 = (s32[]{:T(128)}, f32[32,4,128]{2,0,1:T(8,128)S(1)}, f32[32,4,128]{2,0,1:T(8,128)S(1)}, s32[]{:T(128)}, bf16[8192,4,128]{2,0,1:T(8,128)(2,1)}, /*ind...) while((s32[]{:T(128)}, f32[32,4,128]{2,0,1:T(8,128)S(1)}, ...), condition=%wide.region_18.19_spmd, body=%wide.region_17.18_spmd.sunk | while | flops 67616768 | bytes 3300691 | solution.py:182
  (779 shorter events, 454.2 us)
Async XLA Ops:
  7.2 131.6 %all-gather.5.cloned.1.call-start = ((), (), s32[]{:S(2)}) async-start(), calls=%async_computation | async-start | bytes 8650752 | tf_op jit(solution)/shard_map/all_gather | solution.py:206
  7.9 169.4 %all-gather.7.cloned.1.call-start = ((), (), s32[]{:S(2)}) async-start(), calls=%async_computation.1 | async-start | bytes 8650752 | tf_op jit(solution)/shard_map/all_gather | solution.py:207
  8.6 834.4 %all-gather.9.cloned.1.call-start = ((), (), s32[]{:S(2)}) async-start(), calls=%async_computation.2 | async-start | bytes 8650752 | tf_op jit(solution)/shard_map/all_gather | solution.py:229
  9.4 872.0 %all-gather.11.cloned.1.call-start = ((), (), s32[]{:S(2)}) async-start(), calls=%async_computation.3 | async-start | bytes 8650752 | tf_op jit(solution)/shard_map/all_gather | solution.py:230
  87.1 46.8 %copy-start.1 = (bf16[256,512]{1,0:T(8,128)(2,1)S(1)}, bf16[256,512]{1,0:T(8,128)(2,1)}, u32[]{:S(2)}) copy-start(bf16[256,512]{1,0:T(8,128)(2,1)} %param.22) | copy-start | bytes 786436
  87.1 47.0 %copy-start.2 = (bf16[256,512]{1,0:T(8,128)(2,1)S(1)}, bf16[256,512]{1,0:T(8,128)(2,1)}, u32[]{:S(2)}) copy-start(bf16[256,512]{1,0:T(8,128)(2,1)} %param.23) | copy-start | bytes 786436
  919.8 11.5 copy-start
  919.8 11.5 copy-start.3
  919.8 11.5 copy-start.4
Sparse Core Ops, SparseCore 0:
  9.9 73.7 all-gather.4
  85.6 67.6 all-gather.6
  155.1 67.9 all-gather.8
  224.8 68.1 all-gather.10
where the time goes:
time: 1310 us; the launch traced here: 1300 us
  blocking collectives  472 us (36%)
  local copies, waits for them, and re-layouts  371 us (28%)
  matrix products  348 us (27%)
  other arithmetic  58.5 us (4%)
  loops' own time  31.6 us (2%)
  between operations  15.2 us (1%)
    all_gather x1, blocking collectives, on_device(): lax.all_gather(stat_lse, 'ctx', axis=0, tiled=True)  419 us
    dot_general x72, matrix products, step(): jnp.einsum('hqk,qhd->khd', grad_scores, query_block, preferred_element_ty...  116 us
    dot_general x72, matrix products, step(): jnp.einsum('qhd,khd->hqk', query_block, key_block, preferred_element_type...  96.6 us
    dot_general x72, matrix products, step(): jnp.einsum('hqk,qhd->khd', soft_probs.astype(jnp.bfloat16), grad_block, p...  90 us
    all_gather x1, blocking collectives, on_device(): lax.all_gather(stat_delta, 'ctx', axis=0, tiled=True)  53.4 us
    gather x1, local copies, waits for them, and re-layouts, on_device(): key_pos_comp = jnp.where(live_slot, key_eff[source], far_away)  45.5 us
    gather x1, local copies, waits for them, and re-layouts, on_device(): query_pos_comp = jnp.where(live_slot, query_eff[source], -1)  45.5 us
    gather x1, local copies, waits for them, and re-layouts, on_device(): key_comp = keys_all[source].reshape(padded, head_count, HD)  38.5 us
  transfers between devices with their start and end apart: 4, of which 0 were waited for; matrix products, arithmetic and copies ran while one was open for 30% of the time, Pallas kernels for 0%

commit v1 on v0

v1 whole, which is shorter than its diff:
```python
import functools

import jax
import jax.numpy as jnp
from jax import lax
from jax.experimental import pallas as pl
from jax.experimental.pallas import tpu as pltpu
from jax.sharding import PartitionSpec as P

HD = 128
NZ, NX, NC = 4, 4, 2
NS = NX * NC
BR = 16
SB = 8
SEG = SB * BR
CAP = 2 * SEG
GROUP = NS * SEG
KEYS = NZ * NC * GROUP
UNIT = NC * 2 * SEG
T = 512
SIZES = (512, 640, 768, 1024)
FAR = 1e30
BIG = 1 << 30
SCALE = HD ** (-0.5)
SCALE2 = SCALE * 1.4426950408889634
MESH = pl.DeviceIdType.MESH
VMEM_BYTES = 56 * 1024 * 1024
SMEM = pl.BlockSpec(memory_space=pltpu.SMEM)
VMEM = pl.BlockSpec(memory_space=pltpu.VMEM)
HBM = pl.BlockSpec(memory_space=pltpu.HBM)
NT = (((1,), (1,)), ((), ()))
NN = (((1,), (0,)), ((), ()))


def dot(a, b, dims):
    return lax.dot_general(a, b, dims, preferred_element_type=jnp.float32)


def place():
    me = lax.axis_index("ctx")
    tp = lax.axis_index("tp")
    return me // (NC * NX), lax.rem(me // NC, NX), lax.rem(me, NC), tp


def ctx_of(z, x, core):
    return (z * NX + x) * NC + core


def cols(i):
    return pl.ds(pl.multiple_of(i * HD, HD), HD)


def remote(src, dst, ssem, rsem, dev):
    return pltpu.make_async_remote_copy(
        src_ref=src, dst_ref=dst, send_sem=ssem, recv_sem=rsem, device_id=dev, device_id_type=MESH
    )


def live_blocks(counts, p, c, j):
    nb = (counts[p * NS + j] + BR - 1) // BR
    return (nb + 1 - lax.rem(c + j, NC)) // 2


def attend_kernel(
    q, k, v, g, counts_hbm,
    kv_out, qg_out, att, st_out, info_out, col_out,
    kvs, qgs, stage, kvp, qgp, stv, info, col, oc, m_ref, l_ref, acc, qpos_ref, counts, table,
    csem, loc, sa, ra, sown, sso, rso, sfw, ssf, rz, rs, sst, rst, sat, rat, lat, okv, oqg, ost,
):
    z, x, core, tp = place()
    here = x * NC + core
    sib = (ctx_of(z, x, 1 - core), tp)
    above = (ctx_of(lax.rem(z + 1, NZ), x, core), tp)
    below = (ctx_of(lax.rem(z + NZ - 1, NZ), x, core), tp)
    has_up = z < NZ - 1
    has_dn = z > 0
    counts_copy = pltpu.make_async_copy(counts_hbm, counts, csem)
    counts_copy.start()
    partners = [(dx, dc) for dx in (0, 1, 3, 2) for dc in range(NC) if dx + dc > 0]

    def mate(dx, dc):
        return lax.rem(x + dx, NX), lax.rem(core + dc, NC)

    srcs = ((k, kvs, 0), (v, kvs, 1), (q, qgs, 0), (g, qgs, 1))
    own_parity = lax.rem(core + here, NC)
    own = []
    for a, (src, dst, part) in enumerate(srcs):
        cp = pltpu.make_async_copy(src.at[:, own_parity, :, cols(x)], dst.at[z, core, here, part], loc.at[a])
        cp.start()
        own.append(cp)

    barrier = pltpu.get_barrier_semaphore()
    for dx, dc in partners:
        px, pc = mate(dx, dc)
        pl.semaphore_signal(barrier, inc=1, device_id=(ctx_of(z, px, pc), tp), device_id_type=MESH)
    for dz in range(1, NZ):
        for pc in range(NC):
            pl.semaphore_signal(
                barrier, inc=1, device_id=(ctx_of(lax.rem(z + dz, NZ), x, pc), tp), device_id_type=MESH
            )
    pl.semaphore_wait(barrier, len(partners) + (NZ - 1) * NC)

    sends = []
    for dx, dc in partners:
        px, pc = mate(dx, dc)
        parity = lax.rem(pc + here, NC)
        for a, (src, dst, part) in enumerate(srcs):
            cp = remote(
                src.at[:, parity, :, cols(px)],
                dst.at[z, pc, here, part],
                sa.at[a, dx, dc],
                ra.at[a, dx, dc],
                (ctx_of(z, px, pc), tp),
            )
            cp.start()
            sends.append(cp)

    lane = lax.broadcasted_iota(jnp.int32, (8, SEG), 1)
    for j in range(NS):
        inside = (2 * (lane // BR) + lax.rem(core + j, NC)) * BR + lax.rem(lane, BR)
        qpos_ref[:, j * SEG : (j + 1) * SEG] = (z * NS + j) * CAP + inside
    m_ref[...] = jnp.full(m_ref.shape, -FAR, jnp.float32)
    l_ref[...] = jnp.zeros_like(l_ref)
    acc[...] = jnp.zeros_like(acc)
    counts_copy.wait()
    wide_lane = lax.broadcasted_iota(jnp.int32, (8, GROUP), 1)
    wide_sub = lax.broadcasted_iota(jnp.int32, (8, GROUP), 0)

    def begins(p, c):
        at = [jnp.int32(0)]
        for j in range(NS):
            at.append(at[-1] + live_blocks(counts, p, c, j))
        return at

    def describe(n, _):
        p, c = n // NC, lax.rem(n, NC)
        at = begins(p, c)

        def source(b, _):
            shift = jnp.int32(0)
            for j in range(1, NS):
                shift = jnp.where(b >= at[j], j * SB - at[j], shift)
            table[n * (GROUP // BR) + b] = jnp.minimum(b + shift, GROUP // BR - 1)
            return 0

        lax.fori_loop(0, GROUP // BR, source, 0)
        start = jnp.zeros_like(wide_lane)
        shift = jnp.zeros_like(wide_lane) + c * BR
        kept = jnp.zeros_like(wide_lane) + counts[p * NS]
        for j in range(1, NS):
            inside = wide_lane >= at[j] * BR
            start = jnp.where(inside, at[j] * BR, start)
            shift = jnp.where(inside, j * CAP + lax.rem(c + j, NC) * BR, shift)
            kept = jnp.where(inside, j * CAP + counts[p * NS + j], kept)
        t = wide_lane - start
        pos = t + (t // BR) * BR + shift
        bias = jnp.where(pos < kept, 0.0, -FAR)
        info[p, c] = jnp.where(wide_sub == 0, bias, (pos + p * (NS * CAP)).astype(jnp.float32))
        return 0


    def pack(buf, dst, p):
        def group(c, _):
            stage[...] = buf[p, c]

            def step(i, _):
                for b in range(8):
                    n = table[(p * NC + c) * (GROUP // BR) + i * 8 + b]
                    j, r = n // SB, lax.rem(n, SB)
                    for part in range(2):
                        dst[p, c, part, i * 8 + b] = stage[j, part, r]
                return 0

            lax.fori_loop(0, GROUP // BR // 8, step, 0)
            return 0

        lax.fori_loop(0, NC, group, 0)

    def chunk(buf, p, c, xs):
        return buf.at[p, c, pl.ds(2 * xs, 2)]

    def unit(p, xs):
        inner = lax.broadcasted_iota(jnp.int32, (SEG, 1), 0)
        ks, vs, keys = [], [], []
        for c in range(NC):
            both = kvs[p, c, pl.ds(2 * xs, 2)]
            ks.append(both[:, 0].reshape(2 * SEG, HD))
            vs.append(both[:, 1].reshape(2 * SEG, HD))
            for jj in range(2):
                inside = (2 * (inner // BR) + (c + jj) % 2) * BR + lax.rem(inner, BR)
                live = inside < counts[p * NS + 2 * xs + jj]
                keys.append(jnp.where(live, (p * NS + 2 * xs + jj) * CAP + inside, BIG))
        kk = jnp.concatenate(ks, axis=0)
        vt = jnp.concatenate(vs, axis=0).T
        key = jnp.concatenate(keys, axis=0)
        s = dot(kk, qgs[z, core, :, 0].reshape(GROUP, HD), NT) * SCALE2
        s = jnp.where(key <= qpos_ref[0:1, :], s, -FAR)
        m = m_ref[0:1, :]
        new = jnp.maximum(m, jnp.max(s, axis=0, keepdims=True))
        pr = jnp.exp2(s - new)
        f = jnp.exp2(m - new)
        m_ref[0:1, :] = new
        l_ref[0:1, :] = l_ref[0:1, :] * f + jnp.sum(pr, axis=0, keepdims=True)
        acc[...] = acc[...] * f + dot(vt, pr.astype(jnp.bfloat16), NN)

    flows = ((kvs, -1, has_up, above), (qgs, 1, has_dn, below))

    def place_of(t):
        m = lax.rem(t, NX)
        return t // NX, m, lax.rem(x + NX - (m + m // 2 - 2 * (m // 3)), NX)

    def own_comm(m):
        _, _, xs = place_of(m)
        dx = lax.rem(x + NX - xs, NX)
        for half, (buf, _, has, dev) in enumerate(flows):
            for part in range(2):
                a = 2 * half + part
                for dc in range(NC):
                    ref = buf.at[z, core, xs * NC + lax.rem(core + dc, NC), part]
                    if dc == 0:

                        @pl.when(m == 0)
                        def _():
                            own[a].wait()

                        @pl.when(m > 0)
                        def _():
                            remote(ref, ref, sa.at[a, dx, dc], ra.at[a, dx, dc], sib).wait_recv()

                    else:
                        remote(ref, ref, sa.at[a, dx, dc], ra.at[a, dx, dc], sib).wait_recv()
            ref = chunk(buf, z, core, xs)

            @pl.when(has)
            def _():
                remote(ref, ref, sown.at[half, m], rz.at[z, m], dev).start()

            remote(ref, ref, sso.at[half, m], rso.at[half, m], sib).start()

    def comm(t):
        d, m, xs = place_of(t)
        for buf, sign, has, dev in flows:
            p = z + sign * (d + 1)

            @pl.when((p >= 0) & (p < NZ))
            def _():
                ref = chunk(buf, p, core, xs)
                remote(ref, ref, sfw.at[p, m], rz.at[p, m], sib).wait_recv()

                @pl.when(has)
                def _():
                    remote(ref, ref, sfw.at[p, m], rz.at[p, m], dev).start()

                remote(ref, ref, ssf.at[p, m], rs.at[p, m], sib).start()

    def work(u, _):
        d, m, xs = place_of(u)

        @pl.when(d == 0)
        def _():
            for half, (buf, _, has, dev) in enumerate(flows):
                ref = chunk(buf, z, 1 - core, xs)
                remote(ref, ref, sso.at[half, m], rso.at[half, m], sib).wait_recv()

        for buf, sign, has, dev in flows:
            p = z + sign * d

            @pl.when((d > 0) & (p >= 0) & (p < NZ))
            def _():
                ref = chunk(buf, p, 1 - core, xs)
                remote(ref, ref, ssf.at[p, m], rs.at[p, m], sib).wait_recv()

        @pl.when(z - d >= 0)
        def _():
            unit(z - d, xs)

        whole = (m == NX - 1) & (d < NZ - 1)

        @pl.when(whole & (z - d >= 0))
        def _():
            pack(kvs, kvp, z - d)

        @pl.when(whole & (z + d < NZ))
        def _():
            pack(qgs, qgp, z + d)

        return 0

    def own_step(m, _):
        own_comm(m)
        describe(2 * m, 0)
        describe(2 * m + 1, 0)
        return 0

    def step(t, _):
        @pl.when(t < (NZ - 1) * NX)
        def _():
            comm(t)

        lax.fori_loop(jnp.where(t < 3, 2 * t, t + 3), jnp.where(t < 3, 2 * t + 2, t + 4), work, 0)
        return 0

    lax.fori_loop(0, NX, own_step, 0)
    lax.fori_loop(0, (NZ - 1) * NX + 1, step, 0)

    sub = lax.broadcasted_iota(jnp.int32, (8, SEG), 0)
    at = begins(z, core)
    packed = jnp.where(wide_sub == 0, FAR, 0.0)
    for j in range(NS):
        rows = slice(j * SEG, (j + 1) * SEG)
        live = qpos_ref[0:1, rows] - (z * NS + j) * CAP < counts[z * NS + j]
        l = l_ref[0:1, rows]
        o = jnp.where(live, acc[:, rows] / l, 0.0).T.astype(jnp.bfloat16)
        oc[j] = o.reshape(SB, BR, HD)
        cot = qgs[z, core, j, 1].reshape(SEG, HD).astype(jnp.float32)
        delta = jnp.sum(o.astype(jnp.float32) * cot, axis=1, keepdims=True)
        lse = jnp.where(live, m_ref[0:1, rows] + jnp.log2(l), FAR)
        both = jnp.where(sub == 0, lse, jnp.broadcast_to(delta, (SEG, HD)).T[:8, :])
        both = jnp.concatenate([both, jnp.zeros((8, GROUP - SEG), jnp.float32)], axis=1)
        inside = (wide_lane >= at[j] * BR) & (wide_lane < at[j + 1] * BR)
        packed = jnp.where(inside, pltpu.roll(both, at[j] * BR, 1), packed)
    stv[z, core] = packed
    for j in range(NS):
        rows = slice(j * SEG, (j + 1) * SEG)
        block = jnp.concatenate([packed[:, rows], jnp.zeros((SEG - 8, SEG), jnp.float32)], axis=0)
        col[rows, :] = block.T

    stats = stv.at[z, core]
    remote(stats, stats, sst.at[0], rst.at[z, core], sib).start()
    for dz in range(1, NZ):

        @pl.when(z - dz >= 0)
        def _():
            for pc in range(NC):
                dev = (ctx_of(z - dz, x, pc), tp)
                remote(stats, stats, sst.at[dz * NC + pc], rst.at[z, core], dev).start()

    returns = []
    for dx, dc in partners:
        px, pc = mate(dx, dc)
        there = px * NC + pc
        parity = lax.rem(core + there, NC)
        cp = remote(
            oc.at[there], att.at[x, :, parity], sat.at[dx, dc], rat.at[dx, dc], (ctx_of(z, px, pc), tp)
        )
        cp.start()
        returns.append(cp)
    stay = pltpu.make_async_copy(oc.at[here], att.at[x, :, own_parity], lat)
    stay.start()

    @pl.when(z == NZ - 1)
    def _():
        pack(kvs, kvp, 0)

    @pl.when(z == 0)
    def _():
        pack(qgs, qgp, NZ - 1)

    outs = [
        pltpu.make_async_copy(col, col_out, ost.at[NZ, 0]),
        pltpu.make_async_copy(info, info_out, ost.at[NZ, 1]),
    ]
    for buf, dst, sem in ((kvp, kv_out, okv), (qgp, qg_out, oqg)):
        outs.append(pltpu.make_async_copy(buf.at[z], dst.at[z], sem.at[z]))
    for cp in outs:
        cp.start()
    for dz in range(1, NZ):

        @pl.when(z - dz >= 0)
        def _():
            pltpu.make_async_copy(kvp.at[z - dz], kv_out.at[z - dz], okv.at[z - dz]).start()

        @pl.when(z + dz < NZ)
        def _():
            pltpu.make_async_copy(qgp.at[z + dz], qg_out.at[z + dz], oqg.at[z + dz]).start()

    pltpu.make_async_copy(stats, st_out.at[z, core], ost.at[z, core]).start()

    def take(p, c):
        ref = stv.at[p, c]
        remote(ref, ref, sst.at[0], rst.at[p, c], sib).wait_recv()
        pltpu.make_async_copy(ref, st_out.at[p, c], ost.at[p, c]).start()

    take(z, 1 - core)
    for dz in range(1, NZ):

        @pl.when(z + dz < NZ)
        def _():
            for c in range(NC):
                take(z + dz, c)

    for cp in outs:
        cp.wait()
    stay.wait()
    for dx, dc in partners:
        ox, oc_ = lax.rem(x + NX - dx, NX), lax.rem(core + NC - dc, NC)
        parity = lax.rem(oc_ + here, NC)
        ref = att.at[ox, :, parity]
        remote(oc.at[here], ref, sat.at[dx, dc], rat.at[dx, dc], sib).wait_recv()
    for cp in sends + returns:
        cp.wait_send()
    for c in range(NC):
        pltpu.make_async_copy(stv.at[z, c], st_out.at[z, c], ost.at[z, c]).wait()
    remote(stats, stats, sst.at[0], rst.at[z, core], sib).wait_send()
    for dz in range(1, NZ):

        @pl.when(z - dz >= 0)
        def _():
            pltpu.make_async_copy(kvp.at[z - dz], kv_out.at[z - dz], okv.at[z - dz]).wait()
            for pc in range(NC):
                dev = (ctx_of(z - dz, x, pc), tp)
                remote(stats, stats, sst.at[dz * NC + pc], rst.at[z, core], dev).wait_send()

        @pl.when(z + dz < NZ)
        def _():
            pltpu.make_async_copy(qgp.at[z + dz], qg_out.at[z + dz], oqg.at[z + dz]).wait()
            for c in range(NC):
                pltpu.make_async_copy(stv.at[z + dz, c], st_out.at[z + dz, c], ost.at[z + dz, c]).wait()

    for m in range(NX):
        _, _, xs = place_of(jnp.int32(m))
        for half, (buf, _, has, dev) in enumerate(flows):
            ref = chunk(buf, z, core, xs)

            @pl.when(has)
            def _():
                remote(ref, ref, sown.at[half, m], rz.at[z, m], dev).wait_send()

            remote(ref, ref, sso.at[half, m], rso.at[half, m], sib).wait_send()

    def sent(t, _):
        d, m, xs = place_of(t)
        for buf, sign, has, dev in flows:
            p = z + sign * (d + 1)

            @pl.when((p >= 0) & (p < NZ))
            def _():
                ref = chunk(buf, p, core, xs)

                @pl.when(has)
                def _():
                    remote(ref, ref, sfw.at[p, m], rz.at[p, m], dev).wait_send()

                remote(ref, ref, ssf.at[p, m], rs.at[p, m], sib).wait_send()

        return 0

    lax.fori_loop(0, (NZ - 1) * NX, sent, 0)


WHOLE = (NZ, NC, NS, 2, SB, BR, HD)
PACKED = (NZ, NC, 2, GROUP // BR, BR, HD)
ROWS = (NZ, NC, 8, GROUP)
LANDED = jax.ShapeDtypeStruct((NX, SB, 2, BR, HD), jnp.bfloat16)


def attend(q, k, v, g, counts):
    dma = pltpu.SemaphoreType.DMA
    packed = jax.ShapeDtypeStruct(PACKED, jnp.bfloat16)
    rows = jax.ShapeDtypeStruct(ROWS, jnp.float32)
    return pl.pallas_call(
        attend_kernel,
        out_shape=(
            packed,
            packed,
            LANDED,
            rows,
            rows,
            jax.ShapeDtypeStruct((GROUP, HD), jnp.float32),
        ),
        in_specs=[HBM] * 5,
        out_specs=(HBM,) * 6,
        scratch_shapes=[
            pltpu.VMEM(WHOLE, jnp.bfloat16),
            pltpu.VMEM(WHOLE, jnp.bfloat16),
            pltpu.VMEM((NS, 2, SB, BR, HD), jnp.bfloat16),
            pltpu.VMEM(PACKED, jnp.bfloat16),
            pltpu.VMEM(PACKED, jnp.bfloat16),
            pltpu.VMEM(ROWS, jnp.float32),
            pltpu.VMEM(ROWS, jnp.float32),
            pltpu.VMEM((GROUP, HD), jnp.float32),
            pltpu.VMEM((NS, SB, BR, HD), jnp.bfloat16),
            pltpu.VMEM((8, GROUP), jnp.float32),
            pltpu.VMEM((8, GROUP), jnp.float32),
            pltpu.VMEM((HD, GROUP), jnp.float32),
            pltpu.VMEM((8, GROUP), jnp.int32),
            pltpu.SMEM((NZ * NS,), jnp.int32),
            pltpu.SMEM((NZ * NC * (GROUP // BR),), jnp.int32),
            dma,
            dma((4,)),
            dma((4, NX, NC)),
            dma((4, NX, NC)),
            dma((2, NX)),
            dma((2, NX)),
            dma((2, NX)),
            dma((NZ, NX)),
            dma((NZ, NX)),
            dma((NZ, NX)),
            dma((NZ, NX)),
            dma((NZ * NC,)),
            dma((NZ, NC)),
            dma((NX, NC)),
            dma((NX, NC)),
            dma,
            dma((NZ,)),
            dma((NZ,)),
            dma((NZ + 1, NC)),
        ],
        compiler_params=pltpu.CompilerParams(
            collective_id=0, has_side_effects=True, vmem_limit_bytes=VMEM_BYTES
        ),
        name="attend",
    )(q, k, v, g, counts)


def return_kernel(count, *refs):
    ins, outs = refs[:count], refs[count : 2 * count]
    loc, ssem, rsem = refs[2 * count :]
    z, x, core, tp = place()
    here = x * NC + core
    partners = [(dx, dc) for dx in (2, 1, 3, 0) for dc in range(NC) if dx + dc > 0]
    own = []
    for a in range(count):
        cp = pltpu.make_async_copy(ins[a].at[here], outs[a].at[x, :, lax.rem(core + here, NC)], loc.at[a])
        cp.start()
        own.append(cp)
    barrier = pltpu.get_barrier_semaphore()
    for dx, dc in partners:
        dev = (ctx_of(z, lax.rem(x + dx, NX), lax.rem(core + dc, NC)), tp)
        pl.semaphore_signal(barrier, inc=1, device_id=dev, device_id_type=MESH)
    pl.semaphore_wait(barrier, len(partners))
    sends = []
    for dx, dc in partners:
        px, pc = lax.rem(x + dx, NX), lax.rem(core + dc, NC)
        there = px * NC + pc
        for a in range(count):
            cp = remote(
                ins[a].at[there],
                outs[a].at[x, :, lax.rem(core + there, NC)],
                ssem.at[a, dx, dc],
                rsem.at[a, dx, dc],
                (ctx_of(z, px, pc), tp),
            )
            cp.start()
            sends.append(cp)
    for cp in own:
        cp.wait()
    for dx, dc in partners:
        ox, oc = lax.rem(x + NX - dx, NX), lax.rem(core + NC - dc, NC)
        for a in range(count):
            ref = outs[a].at[ox, :, lax.rem(oc + here, NC)]
            remote(
                ins[a].at[here], ref, ssem.at[a, dx, dc], rsem.at[a, dx, dc], (ctx_of(z, ox, oc), tp)
            ).wait_recv()
    for cp in sends:
        cp.wait_send()


def return_heads(*arrays):
    count = len(arrays)
    dma = pltpu.SemaphoreType.DMA
    return pl.pallas_call(
        functools.partial(return_kernel, count),
        out_shape=(LANDED,) * count,
        in_specs=[HBM] * count,
        out_specs=(HBM,) * count,
        scratch_shapes=[dma((count,)), dma((count, NX, NC)), dma((count, NX, NC))],
        compiler_params=pltpu.CompilerParams(collective_id=1, has_side_effects=True),
        name="return_heads",
    )(*arrays)


def assemble_kernel(count, *refs):
    ins, outs = refs[:count], refs[count : 2 * count]
    bufs, res, lsem, ssem = refs[2 * count : 2 * count + 4]
    loads = [pltpu.make_async_copy(ins[a], bufs.at[a], lsem.at[a]) for a in range(count)]
    stores = [pltpu.make_async_copy(res.at[a], outs[a], ssem.at[a]) for a in range(count)]
    for cp in loads:
        cp.start()
    for a in range(count):
        loads[a].wait()
        for i in range(NX):
            res[a, :, i * HD : (i + 1) * HD] = bufs[a, i].reshape(CAP, HD)
        stores[a].start()
    for cp in stores:
        cp.wait()


def assemble(*arrays):
    count = len(arrays)
    dma = pltpu.SemaphoreType.DMA
    shape = jax.ShapeDtypeStruct((CAP, NX * HD), jnp.bfloat16)
    return pl.pallas_call(
        functools.partial(assemble_kernel, count),
        out_shape=(shape,) * count,
        in_specs=[HBM] * count,
        out_specs=(HBM,) * count,
        scratch_shapes=[
            pltpu.VMEM((count,) + LANDED.shape, jnp.bfloat16),
            pltpu.VMEM((count, CAP, NX * HD), jnp.bfloat16),
            dma((count,)),
            dma((count,)),
        ],
        compiler_params=pltpu.CompilerParams(vmem_limit_bytes=VMEM_BYTES),
        name="assemble",
    )(*arrays)


def fill_offsets(counts, off, z, sign, planes):
    def step(n, at):
        off[n] = at
        p, c = z + sign * (n // NC), lax.rem(n, NC)
        for j in range(NS):
            at = at + live_blocks(counts, p, c, j)
        return at

    off[planes * NC] = lax.fori_loop(0, planes * NC, step, jnp.int32(0))


def load(off, src, dst, sem, z, sign, planes, wait):
    def step(n, _):
        at = off[n]
        blocks = off[n + 1] - at
        cp = pltpu.make_async_copy(
            src.at[z + sign * (n // NC), lax.rem(n, NC), :, pl.ds(0, blocks)],
            dst.at[:, pl.ds(at, blocks)],
            sem.at[n],
        )
        if wait:
            cp.wait()
        else:
            cp.start()
        return 0

    lax.fori_loop(0, planes * NC, step, 0)


def line_up(off, src, dst, z, sign, planes, tail):
    width = GROUP + 128
    lane = lax.broadcasted_iota(jnp.int32, (8, width), 1)
    sub = lax.broadcasted_iota(jnp.int32, (8, 128), 0)

    def step(n, _):
        to = off[n] * BR
        at = pl.multiple_of((to // 128) * 128, 128)
        new = src[z + sign * (n // NC), lax.rem(n, NC)]
        new = pltpu.roll(jnp.concatenate([new, jnp.zeros((8, 128), jnp.float32)], axis=1), to - at, 1)
        old = dst[:, pl.ds(at, width)]
        dst[:, pl.ds(at, width)] = jnp.where(lane >= to - at, new, old)
        return 0

    lax.fori_loop(0, planes * NC, step, 0)
    total = off[planes * NC] * BR
    blank = jnp.where(sub == 0, tail, 0.0)
    for t in range(T // 128 + 1):
        at = pl.multiple_of((total // 128 + t) * 128, 128)
        old = dst[:, pl.ds(at, 128)]
        dst[:, pl.ds(at, 128)] = jnp.where(at + lane[:, :128] >= total, blank, old)


def backward_kernel(
    counts_hbm, qg, kv, st, info, stcol, dq_out, dk_out, dv_out,
    counts, koff, qoff, kvc, qgc, stv, infov, qrow, krow, col, dqa, dka, dva, res,
    csem, ksem, qsem, ssem, osem,
):
    z, x, core, _ = place()
    cp = pltpu.make_async_copy(counts_hbm, counts, csem)
    cp.start()
    smalls = [
        pltpu.make_async_copy(src, dst, ssem.at[i])
        for i, (src, dst) in enumerate(((st, stv), (info, infov), (stcol, col)))
    ]
    for small in smalls:
        small.start()
    cp.wait()
    kplanes, qplanes = z + 1, NZ - z
    fill_offsets(counts, koff, z, -1, kplanes)
    load(koff, kv, kvc, ksem, z, -1, kplanes, False)
    fill_offsets(counts, qoff, z, 1, qplanes)
    load(qoff, qg, qgc, qsem, z, 1, qplanes, False)
    key_end = koff[kplanes * NC]
    query_end = qoff[qplanes * NC]
    plane_end = koff[NC]
    zero = jnp.zeros((GROUP // BR, BR, HD), jnp.bfloat16)
    for part in range(2):
        kvc[part, pl.ds(key_end, GROUP // BR)] = zero
        qgc[part, pl.ds(query_end, GROUP // BR)] = zero
    for small in smalls:
        small.wait()
    line_up(koff, infov, krow, z, -1, kplanes, -FAR)
    line_up(qoff, stv, qrow, z, 1, qplanes, FAR)
    base = koff[core]
    total = koff[core + 1] - base
    starts = [jnp.int32(0)]
    for j in range(NS):
        starts.append(starts[-1] + live_blocks(counts, z, core, j))
    load(koff, kv, kvc, ksem, z, -1, kplanes, True)
    load(qoff, qg, qgc, qsem, z, 1, qplanes, True)

    def tile(buf, part, t):
        return buf[part, pl.ds(t * (T // BR), T // BR)].reshape(T, HD)

    def run(M):
        rows = pl.ds(base, M // BR)
        r = lax.broadcasted_iota(jnp.int32, (M, 1), 0)
        start = jnp.zeros_like(r)
        shift = jnp.zeros_like(r) + lax.rem(core, NC) * BR
        for j in range(1, NS):
            inside = r >= starts[j] * BR
            start = jnp.where(inside, starts[j] * BR, start)
            shift = jnp.where(inside, j * CAP + lax.rem(core + j, NC) * BR, shift)
        t = r - start
        pos = (t + (t // BR) * BR + shift + z * (NS * CAP)).astype(jnp.float32)

        dka[0:M, :] = jnp.zeros((M, HD), jnp.float32)
        dva[0:M, :] = jnp.zeros((M, HD), jnp.float32)
        dqa[0:M, :] = jnp.zeros((M, HD), jnp.float32)

        def key_step(qt, _):
            lanes = pl.ds(pl.multiple_of(qt * T, T), T)
            qb, gb = tile(qgc, 0, qt), tile(qgc, 1, qt)
            p = jnp.exp2(dot(kvc[0, rows].reshape(M, HD), qb, NT) * SCALE2 - qrow[0:1, lanes])
            n = qt * T + lax.broadcasted_iota(jnp.int32, (1, T), 1)
            there = jnp.where(n < plane_end * BR, krow[1:2, lanes], FAR)
            p = jnp.where(pos <= there, p, 0.0)
            dva[0:M, :] += dot(p.astype(jnp.bfloat16), gb, NN)
            dp = dot(kvc[1, rows].reshape(M, HD), gb, NT)
            ds = (p * (dp - qrow[1:2, lanes])).astype(jnp.bfloat16)
            dka[0:M, :] += dot(ds, qb, NN)
            return 0

        def query_step(kt, _):
            lanes = pl.ds(pl.multiple_of(kt * T, T), T)
            kb, vb = tile(kvc, 0, kt), tile(kvc, 1, kt)
            s = dot(qgc[0, rows].reshape(M, HD), kb, NT) * SCALE2 + krow[0:1, lanes]
            s = jnp.where(krow[1:2, lanes] <= pos, s, -FAR)
            p = jnp.exp2(s - col[0:M, 0:1])
            dp = dot(qgc[1, rows].reshape(M, HD), vb, NT)
            dqa[0:M, :] += dot((p * (dp - col[0:M, 1:2])).astype(jnp.bfloat16), kb, NN)
            return 0

        per = T // BR
        lax.fori_loop(0, (query_end + per - 1) // per, key_step, 0)
        lax.fori_loop(0, (key_end + per - 1) // per, query_step, 0)

    lower = 0
    for size in SIZES:

        @pl.when((total * BR > lower) & (total * BR <= size))
        def _():
            run(size)

        lower = size

    r = lax.broadcasted_iota(jnp.int32, (SEG, HD), 0)
    stores = []
    for a, (src, dst, scale) in enumerate(((dka, dk_out, SCALE), (dva, dv_out, 1.0), (dqa, dq_out, SCALE))):
        for j in range(NS):
            row = r + (r // BR + lax.rem(core + j, NC)) * BR
            part = src[pl.ds(pl.multiple_of(starts[j] * BR, BR), SEG), :] * scale
            part = jnp.where(row < counts[z * NS + j], part, 0.0)
            res[a, j] = part.astype(jnp.bfloat16).reshape(SB, BR, HD)
        cp = pltpu.make_async_copy(res.at[a], dst, osem.at[a])
        cp.start()
        stores.append(cp)
    for cp in stores:
        cp.wait()


def backward(counts, qg, kv, st, info, stcol):
    dma = pltpu.SemaphoreType.DMA
    parts = jax.ShapeDtypeStruct((NS, SB, BR, HD), jnp.bfloat16)
    blocks = (KEYS + GROUP + T) // BR
    return pl.pallas_call(
        backward_kernel,
        out_shape=(parts, parts, parts),
        in_specs=[HBM] * 6,
        out_specs=(HBM,) * 3,
        scratch_shapes=[
            pltpu.SMEM((NZ * NS,), jnp.int32),
            pltpu.SMEM((NZ * NC + 1,), jnp.int32),
            pltpu.SMEM((NZ * NC + 1,), jnp.int32),
            pltpu.VMEM((2, blocks, BR, HD), jnp.bfloat16),
            pltpu.VMEM((2, blocks, BR, HD), jnp.bfloat16),
            pltpu.VMEM(ROWS, jnp.float32),
            pltpu.VMEM(ROWS, jnp.float32),
            pltpu.VMEM((8, KEYS + GROUP + T), jnp.float32),
            pltpu.VMEM((8, KEYS + GROUP + T), jnp.float32),
            pltpu.VMEM((GROUP, HD), jnp.float32),
            pltpu.VMEM((GROUP + SEG, HD), jnp.float32),
            pltpu.VMEM((GROUP + SEG, HD), jnp.float32),
            pltpu.VMEM((GROUP + SEG, HD), jnp.float32),
            pltpu.VMEM((3, NS, SB, BR, HD), jnp.bfloat16),
            dma,
            dma((NZ * NC,)),
            dma((NZ * NC,)),
            dma((3,)),
            dma((3,)),
        ],
        compiler_params=pltpu.CompilerParams(vmem_limit_bytes=VMEM_BYTES),
        name="backward",
    )(counts, qg, kv, st, info, stcol)


def on_device(query_heads, key_heads, value_heads, grad_heads, counts):
    def blocks(array):
        return array.reshape(SB, 2, BR, NX * HD)

    kv, qg, att, st, info, stcol = attend(
        blocks(query_heads), blocks(key_heads), blocks(value_heads), blocks(grad_heads), counts
    )
    dq, dk, dv = backward(counts, qg, kv, st, info, stcol)
    return assemble(att, *return_heads(dq, dk, dv))


def solution(mesh):
    return jax.shard_map(
        on_device,
        mesh=mesh,
        in_specs=(P("ctx", "tp"), P("ctx", "tp"), P("ctx", "tp"), P("ctx", "tp"), P()),
        out_specs=(P("ctx", "tp"), P("ctx", "tp"), P("ctx", "tp"), P("ctx", "tp")),
        check_vma=False,
    )
```

time: 1310 us -> 92 us (0.07)
  the two profiles are of different devices: /device:TPU:1 before, /device:TPU:33 now
where the time goes in v1:
time: 92 us; the launch traced here: 91.9 us
  Pallas kernels  91.1 us (99%)
    pallas_call x1, Pallas kernels, attend(): pl.pallas_call(attend_kernel, out_shape=(packed, packed, LANDED, rows, ro...  56.8 us
    pallas_call x1, Pallas kernels, backward(): pl.pallas_call(backward_kernel, out_shape=(parts, parts, parts), in_specs...  19.1 us
    pallas_call x1, Pallas kernels, return_heads(): pl.pallas_call(functools.partial(return_kernel, count), out_shape=(LANDED...  13.1 us
    pallas_call x1, Pallas kernels, assemble(): pl.pallas_call(functools.partial(assemble_kernel, count), out_shape=(shap...  2.03 us

profile of v1, /device:TPU:33, one launch (start us, length us, event | category | flops | bytes accessed | tf_op | source)
XLA Modules:
  0.0 91.9 jit_solution(16641106402104473608)
XLA Ops:
  0.6 56.8 %attend.1 = (bf16[4,2,2,64,16,128]{5,4,3,2,1,0:T(8,128)(2,1)}, bf16[4,2,2,64,16,128]{5,4,3,2,1,0:T(8,128)(2,1)}, bf16[4,8,2,16,128]{4,3,2,1,0:T(8,128)(2,1)}, f3...) custom-call(bf16[8,2,16,512]{3,2,1,0:T(8,128)(2,1)} %bitcast.4, ...), custom_call_target="tpu_custom_call" | custom-call | tf_op jit(solution)/shard_map/attend/pallas_call | solution.py:461
  57.5 19.1 %backward.1 = (bf16[8,8,16,128]{3,2,1,0:T(8,128)(2,1)}, bf16[8,8,16,128]{3,2,1,0:T(8,128)(2,1)}, bf16[8,8,16,128]{3,2,1,0:T(8,128)(2,1)}) custom-call(s32[32]{0:T(128)} %counts_hbm.3, bf16[4,2,2,64,16,128]{5,4,3,2,1,0:T(8,128)(2,1)} %get-tuple-element.17.qg, bf16[4,2,2,64,16,128]{5,4,3,2,1,0:T(8,128)(2,1)} %get-tuple-element.18.kv, ...), custom_call_target="tpu_custom_call" | custom-call | tf_op jit(solution)/shard_map/backward/pallas_call | solution.py:774
  76.6 13.1 %return_heads.1 = (bf16[4,8,2,16,128]{4,3,2,1,0:T(8,128)(2,1)}, bf16[4,8,2,16,128]{4,3,2,1,0:T(8,128)(2,1)}, bf16[4,8,2,16,128]{4,3,2,1,0:T(8,128)(2,1)}) custom-call(bf16[8,8,16,128]{3,2,1,0:T(8,128)(2,1)} %get-tuple-element.22.refs_0_, bf16[8,8,16,128]{3,2,1,0:T(8,128)(2,1)} %get-tuple-element.23.refs_1_, bf16[8,8,16,128]{3,2,1,0:T(8,128)(2,1)} %get-tuple-element.24.refs_2_), custom_call_target="tpu_custom_call" | custom-call | tf_op jit(solution)/shard_map/return_heads/pallas_call | solution.py:562
  89.7 2.0 %assemble.1 = (bf16[256,512]{1,0:T(8,128)(2,1)}, bf16[256,512]{1,0:T(8,128)(2,1)}, bf16[256,512]{1,0:T(8,128)(2,1)}, bf16[256,512]{1,0:T(8,128)(2,1)}) custom-call(bf16[4,8,2,16,128]{4,3,2,1,0:T(8,128)(2,1)} %get-tuple-element.16.refs_0_, bf16[4,8,2,16,128]{4,3,2,1,0:T(8,128)(2,1)} %get-tuple-element.25.refs_1_, ...), custom_call_target="tpu_custom_call" | custom-call | tf_op jit(solution)/shard_map/assemble/pallas_call | solution.py:593

commit v2 on v1

--- a/solution.py
+++ b/solution.py
@@ -18,7 +18,7 @@
 KEYS = NZ * NC * GROUP
 UNIT = NC * 2 * SEG
 T = 512
-SIZES = (512, 640, 768, 1024)
+SIZES = (640, 768, 1024)
 FAR = 1e30
 BIG = 1 << 30
 SCALE = HD ** (-0.5)
@@ -63,9 +63,9 @@
 
 def attend_kernel(
     q, k, v, g, counts_hbm,
-    kv_out, qg_out, att, st_out, info_out, col_out,
-    kvs, qgs, stage, kvp, qgp, stv, info, col, oc, m_ref, l_ref, acc, qpos_ref, counts, table,
-    csem, loc, sa, ra, sown, sso, rso, sfw, ssf, rz, rs, sst, rst, sat, rat, lat, okv, oqg, ost,
+    kv_out, qg_out, att, st_out, info_out, col_out, dq_out, dkv_out,
+    kvs, qgs, stage, dqs, dkv, kvp, qgp, stv, info, col, oc, m_ref, l_ref, acc, qpos_ref, counts, table,
+    csem, loc, sa, ra, sown, sso, rso, sfw, ssf, rz, rs, sst, rst, sat, rat, lat, okv, oqg, ost, sdq, sdkv,
 ):
     z, x, core, tp = place()
     here = x * NC + core
@@ -122,6 +122,7 @@
     m_ref[...] = jnp.full(m_ref.shape, -FAR, jnp.float32)
     l_ref[...] = jnp.zeros_like(l_ref)
     acc[...] = jnp.zeros_like(acc)
+    dkv[...] = jnp.zeros_like(dkv)
     counts_copy.wait()
     wide_lane = lax.broadcasted_iota(jnp.int32, (8, GROUP), 1)
     wide_sub = lax.broadcasted_iota(jnp.int32, (8, GROUP), 0)
@@ -179,7 +180,7 @@
     def chunk(buf, p, c, xs):
         return buf.at[p, c, pl.ds(2 * xs, 2)]
 
-    def unit(p, xs):
+    def keys_of(p, xs):
         inner = lax.broadcasted_iota(jnp.int32, (SEG, 1), 0)
         ks, vs, keys = [], [], []
         for c in range(NC):
@@ -191,17 +192,51 @@
                 live = inside < counts[p * NS + 2 * xs + jj]
                 keys.append(jnp.where(live, (p * NS + 2 * xs + jj) * CAP + inside, BIG))
         kk = jnp.concatenate(ks, axis=0)
-        vt = jnp.concatenate(vs, axis=0).T
-        key = jnp.concatenate(keys, axis=0)
+        vv = jnp.concatenate(vs, axis=0)
         s = dot(kk, qgs[z, core, :, 0].reshape(GROUP, HD), NT) * SCALE2
-        s = jnp.where(key <= qpos_ref[0:1, :], s, -FAR)
+        return kk, vv, jnp.where(jnp.concatenate(keys, axis=0) <= qpos_ref[0:1, :], s, -FAR)
+
+    def unit(p, xs):
+        _, vv, s = keys_of(p, xs)
         m = m_ref[0:1, :]
         new = jnp.maximum(m, jnp.max(s, axis=0, keepdims=True))
         pr = jnp.exp2(s - new)
         f = jnp.exp2(m - new)
         m_ref[0:1, :] = new
         l_ref[0:1, :] = l_ref[0:1, :] * f + jnp.sum(pr, axis=0, keepdims=True)
-        acc[...] = acc[...] * f + dot(vt, pr.astype(jnp.bfloat16), NN)
+        acc[...] = acc[...] * f + dot(vv.T, pr.astype(jnp.bfloat16), NN)
+
+    def unit_back(p, xs):
+        kk, vv, s = keys_of(p, xs)
+        pr = jnp.exp2(s - m_ref[0:1, :])
+        dp = dot(vv, qgs[z, core, :, 1].reshape(GROUP, HD), NT)
+        ds = (pr * (dp - l_ref[0:1, :])).astype(jnp.bfloat16)
+        acc[...] += dot(kk.T, ds, NN)
+
+    def unit_key(p, xs):
+        line = lax.broadcasted_iota(jnp.int32, (1, SEG), 1)
+        inner = lax.broadcasted_iota(jnp.int32, (SEG, 1), 0)
+        qs, gs, lses, deltas, queries, keys = [], [], [], [], [], []
+        for c in range(NC):
+            both = qgs[p, c, pl.ds(2 * xs, 2)]
+            qs.append(both[:, 0].reshape(2 * SEG, HD))
+            gs.append(both[:, 1].reshape(2 * SEG, HD))
+            lanes = pl.ds(pl.multiple_of(2 * xs * SEG, 2 * SEG), 2 * SEG)
+            lses.append(stv[p, c, 2:3, lanes])
+            deltas.append(stv[p, c, 3:4, lanes])
+            for jj in range(2):
+                inside = (2 * (line // BR) + (c + jj) % 2) * BR + lax.rem(line, BR)
+                queries.append((p * NS + 2 * xs + jj) * CAP + inside)
+        for j in range(NS):
+            keys.append(j * CAP + (2 * (inner // BR) + lax.rem(core + j, NC)) * BR + lax.rem(inner, BR))
+        qq, gg = jnp.concatenate(qs, axis=0), jnp.concatenate(gs, axis=0)
+        lse, delta = jnp.concatenate(lses, axis=1), jnp.concatenate(deltas, axis=1)
+        s = dot(kvs[0, core, :, 0].reshape(GROUP, HD), qq, NT) * SCALE2
+        pr = jnp.exp2(s - lse)
+        pr = jnp.where(jnp.concatenate(keys, axis=0) <= jnp.concatenate(queries, axis=1), pr, 0.0)
+        dkv[1] += dot(pr.astype(jnp.bfloat16), gg, NN)
+        dp = dot(kvs[0, core, :, 1].reshape(GROUP, HD), gg, NT)
+        dkv[0] += dot((pr * (dp - delta)).astype(jnp.bfloat16), qq, NN)
 
     flows = ((kvs, -1, has_up, above), (qgs, 1, has_dn, below))
 
@@ -276,11 +311,11 @@
 
         whole = (m == NX - 1) & (d < NZ - 1)
 
-        @pl.when(whole & (z - d >= 0))
+        @pl.when(whole & ((d == 0) | (z == NZ - 1)))
         def _():
             pack(kvs, kvp, z - d)
 
-        @pl.when(whole & (z + d < NZ))
+        @pl.when(whole & (z > 0) & (z + d < NZ))
         def _():
             pack(qgs, qgp, z + d)
 
@@ -292,61 +327,119 @@
         describe(2 * m + 1, 0)
         return 0
 
+    stats = stv.at[z, core]
+
+    def send_stats(act):
+        act(remote(stats, stats, sst.at[0], rst.at[z, core], sib))
+        for dz in range(1, NZ):
+
+            @pl.when(z - dz >= 0)
+            def _():
+                for pc in range(NC):
+                    dev = (ctx_of(z - dz, x, pc), tp)
+                    act(remote(stats, stats, sst.at[dz * NC + pc], rst.at[z, core], dev))
+
+    def send_rows(act):
+        for dx, dc in partners:
+            px, pc = mate(dx, dc)
+            there = px * NC + pc
+            parity = lax.rem(core + there, NC)
+            act(
+                remote(
+                    oc.at[there], att.at[x, :, parity], sat.at[dx, dc], rat.at[dx, dc], (ctx_of(z, px, pc), tp)
+                )
+            )
+
+    stay = pltpu.make_async_copy(oc.at[here], att.at[x, :, own_parity], lat)
+
+    def finish():
+        sub = lax.broadcasted_iota(jnp.int32, (8, SEG), 0)
+        at = begins(z, core)
+        packed = jnp.where(wide_sub == 0, FAR, 0.0)
+        for j in range(NS):
+            rows = slice(j * SEG, (j + 1) * SEG)
+            live = qpos_ref[0:1, rows] - (z * NS + j) * CAP < counts[z * NS + j]
+            l = l_ref[0:1, rows]
+            o = jnp.where(live, acc[:, rows] / l, 0.0).T.astype(jnp.bfloat16)
+            oc[j] = o.reshape(SB, BR, HD)
+            cot = qgs[z, core, j, 1].reshape(SEG, HD).astype(jnp.float32)
+            delta = jnp.sum(o.astype(jnp.float32) * cot, axis=1, keepdims=True)
+            lse = jnp.where(live, m_ref[0:1, rows] + jnp.log2(l), FAR)
+            both = jnp.where(sub == 0, lse, jnp.broadcast_to(delta, (SEG, HD)).T[:8, :])
+            m_ref[0:1, rows] = lse
+            l_ref[0:1, rows] = both[1:2, :]
+            both = jnp.concatenate([both, jnp.zeros((8, GROUP - SEG), jnp.float32)], axis=1)
+            inside = (wide_lane >= at[j] * BR) & (wide_lane < at[j + 1] * BR)
+            packed = jnp.where(inside, pltpu.roll(both, at[j] * BR, 1), packed)
+        dense = jnp.where(wide_sub == 2, m_ref[0:1, :], l_ref[0:1, :])
+        stv[z, core] = jnp.where(wide_sub < 2, packed, dense)
+        for j in range(NS):
+            rows = slice(j * SEG, (j + 1) * SEG)
+            block = jnp.concatenate([packed[:, rows], jnp.zeros((SEG - 8, SEG), jnp.float32)], axis=0)
+            col[rows, :] = block.T
+
+        acc[...] = jnp.zeros_like(acc)
+        send_stats(lambda cp: cp.start())
+        send_rows(lambda cp: cp.start())
+        stay.start()
+
+    top = z == NZ - 1
+    done = jnp.where(z == 0, 1, 4 * z)
+    pace = jnp.where(z == NZ - 2, 3, 1)
+
+    def back(u, _):
+        d, m, xs = place_of(u)
+        unit_back(z - d, xs)
+        return 0
+
+    def key_work(w, _):
+        p, m, xs = place_of(w)
+        for c in range(NC):
+
+            @pl.when((m == 0) & ((p > 0) | (c != core)))
+            def _():
+                ref = stv.at[p, c]
+                remote(ref, ref, sst.at[0], rst.at[p, c], sib).wait_recv()
+
+        unit_key(p, xs)
+        return 0
+
     def step(t, _):
         @pl.when(t < (NZ - 1) * NX)
         def _():
             comm(t)
 
         lax.fori_loop(jnp.where(t < 3, 2 * t, t + 3), jnp.where(t < 3, 2 * t + 2, t + 4), work, 0)
+
+        @pl.when(t == done)
+        def _():
+            finish()
+
+        @pl.when((t > done) & (z < NZ - 1))
+        def _():
+            first = (t - done - 1) * pace
+            last = jnp.minimum(first + pace, NX * (z + 1))
+            lax.fori_loop(first, last, back, 0)
+
+        @pl.when((z == 0) & (t >= 6) & (t < 12))
+        def _():
+            lax.fori_loop(2 * t - 12, 2 * t - 10, key_work, 0)
+
         return 0
 
     lax.fori_loop(0, NX, own_step, 0)
     lax.fori_loop(0, (NZ - 1) * NX + 1, step, 0)
 
-    sub = lax.broadcasted_iota(jnp.int32, (8, SEG), 0)
-    at = begins(z, core)
-    packed = jnp.where(wide_sub == 0, FAR, 0.0)
-    for j in range(NS):
-        rows = slice(j * SEG, (j + 1) * SEG)
-        live = qpos_ref[0:1, rows] - (z * NS + j) * CAP < counts[z * NS + j]
-        l = l_ref[0:1, rows]
-        o = jnp.where(live, acc[:, rows] / l, 0.0).T.astype(jnp.bfloat16)
-        oc[j] = o.reshape(SB, BR, HD)
-        cot = qgs[z, core, j, 1].reshape(SEG, HD).astype(jnp.float32)
-        delta = jnp.sum(o.astype(jnp.float32) * cot, axis=1, keepdims=True)
-        lse = jnp.where(live, m_ref[0:1, rows] + jnp.log2(l), FAR)
-        both = jnp.where(sub == 0, lse, jnp.broadcast_to(delta, (SEG, HD)).T[:8, :])
-        both = jnp.concatenate([both, jnp.zeros((8, GROUP - SEG), jnp.float32)], axis=1)
-        inside = (wide_lane >= at[j] * BR) & (wide_lane < at[j + 1] * BR)
-        packed = jnp.where(inside, pltpu.roll(both, at[j] * BR, 1), packed)
-    stv[z, core] = packed
-    for j in range(NS):
-        rows = slice(j * SEG, (j + 1) * SEG)
-        block = jnp.concatenate([packed[:, rows], jnp.zeros((SEG - 8, SEG), jnp.float32)], axis=0)
-        col[rows, :] = block.T
-
-    stats = stv.at[z, core]
-    remote(stats, stats, sst.at[0], rst.at[z, core], sib).start()
-    for dz in range(1, NZ):
-
-        @pl.when(z - dz >= 0)
-        def _():
-            for pc in range(NC):
-                dev = (ctx_of(z - dz, x, pc), tp)
-                remote(stats, stats, sst.at[dz * NC + pc], rst.at[z, core], dev).start()
-
-    returns = []
-    for dx, dc in partners:
-        px, pc = mate(dx, dc)
-        there = px * NC + pc
-        parity = lax.rem(core + there, NC)
-        cp = remote(
-            oc.at[there], att.at[x, :, parity], sat.at[dx, dc], rat.at[dx, dc], (ctx_of(z, px, pc), tp)
-        )
-        cp.start()
-        returns.append(cp)
-    stay = pltpu.make_async_copy(oc.at[here], att.at[x, :, own_parity], lat)
-    stay.start()
+    @pl.when(z < NZ - 1)
+    def _():
+        for j in range(NS):
+            rows = slice(j * SEG, (j + 1) * SEG)
+            dqs[j] = (acc[:, rows] * SCALE).T.astype(jnp.bfloat16).reshape(SB, BR, HD)
+        pltpu.make_async_copy(dqs, dq_out, sdq).start()
+
+    @pl.when(z == 0)
+    def _():
+        pltpu.make_async_copy(dkv, dkv_out, sdkv).start()
 
     @pl.when(z == NZ - 1)
     def _():
@@ -364,30 +457,35 @@
         outs.append(pltpu.make_async_copy(buf.at[z], dst.at[z], sem.at[z]))
     for cp in outs:
         cp.start()
-    for dz in range(1, NZ):
-
-        @pl.when(z - dz >= 0)
+    def copies(act, take):
+        for dz in range(1, NZ):
+
+            @pl.when((z - dz >= 0) & (z == NZ - 1))
+            def _():
+                act(pltpu.make_async_copy(kvp.at[z - dz], kv_out.at[z - dz], okv.at[z - dz]))
+
+            @pl.when((z + dz < NZ) & ((z > 0) | (dz == NZ - 1)))
+            def _():
+                act(pltpu.make_async_copy(qgp.at[z + dz], qg_out.at[z + dz], oqg.at[z + dz]))
+
+        @pl.when(z > 0)
         def _():
-            pltpu.make_async_copy(kvp.at[z - dz], kv_out.at[z - dz], okv.at[z - dz]).start()
-
-        @pl.when(z + dz < NZ)
-        def _():
-            pltpu.make_async_copy(qgp.at[z + dz], qg_out.at[z + dz], oqg.at[z + dz]).start()
-
-    pltpu.make_async_copy(stats, st_out.at[z, core], ost.at[z, core]).start()
+            act(pltpu.make_async_copy(stats, st_out.at[z, core], ost.at[z, core]))
+            take(z, 1 - core)
+
+        for dz in range(1, NZ):
+
+            @pl.when((z + dz < NZ) & ((z > 0) | (dz == NZ - 1)))
+            def _():
+                for c in range(NC):
+                    take(z + dz, c)
 
     def take(p, c):
         ref = stv.at[p, c]
         remote(ref, ref, sst.at[0], rst.at[p, c], sib).wait_recv()
         pltpu.make_async_copy(ref, st_out.at[p, c], ost.at[p, c]).start()
 
-    take(z, 1 - core)
-    for dz in range(1, NZ):
-
-        @pl.when(z + dz < NZ)
-        def _():
-            for c in range(NC):
-                take(z + dz, c)
+    copies(lambda cp: cp.start(), take)
 
     for cp in outs:
         cp.wait()
@@ -397,25 +495,23 @@
         parity = lax.rem(oc_ + here, NC)
         ref = att.at[ox, :, parity]
         remote(oc.at[here], ref, sat.at[dx, dc], rat.at[dx, dc], sib).wait_recv()
-    for cp in sends + returns:
+    for cp in sends:
         cp.wait_send()
-    for c in range(NC):
-        pltpu.make_async_copy(stv.at[z, c], st_out.at[z, c], ost.at[z, c]).wait()
-    remote(stats, stats, sst.at[0], rst.at[z, core], sib).wait_send()
-    for dz in range(1, NZ):
-
-        @pl.when(z - dz >= 0)
-        def _():
-            pltpu.make_async_copy(kvp.at[z - dz], kv_out.at[z - dz], okv.at[z - dz]).wait()
-            for pc in range(NC):
-                dev = (ctx_of(z - dz, x, pc), tp)
-                remote(stats, stats, sst.at[dz * NC + pc], rst.at[z, core], dev).wait_send()
-
-        @pl.when(z + dz < NZ)
-        def _():
-            pltpu.make_async_copy(qgp.at[z + dz], qg_out.at[z + dz], oqg.at[z + dz]).wait()
-            for c in range(NC):
-                pltpu.make_async_copy(stv.at[z + dz, c], st_out.at[z + dz, c], ost.at[z + dz, c]).wait()
+    send_rows(lambda cp: cp.wait_send())
+    send_stats(lambda cp: cp.wait_send())
+
+    @pl.when(z < NZ - 1)
+    def _():
+        pltpu.make_async_copy(dqs, dq_out, sdq).wait()
+
+    @pl.when(z == 0)
+    def _():
+        pltpu.make_async_copy(dkv, dkv_out, sdkv).wait()
+
+    copies(
+        lambda cp: cp.wait(),
+        lambda p, c: pltpu.make_async_copy(stv.at[p, c], st_out.at[p, c], ost.at[p, c]).wait(),
+    )
 
     for m in range(NX):
         _, _, xs = place_of(jnp.int32(m))
@@ -452,6 +548,9 @@
 PACKED = (NZ, NC, 2, GROUP // BR, BR, HD)
 ROWS = (NZ, NC, 8, GROUP)
 LANDED = jax.ShapeDtypeStruct((NX, SB, 2, BR, HD), jnp.bfloat16)
+PARTS = jax.ShapeDtypeStruct((NS, SB, BR, HD), jnp.bfloat16)
+GRADS = jax.ShapeDtypeStruct((NS, 3, SB, BR, HD), jnp.bfloat16)
+LANDED3 = jax.ShapeDtypeStruct((NX, 3, SB, 2, BR, HD), jnp.bfloat16)
 
 
 def attend(q, k, v, g, counts):
@@ -467,13 +566,17 @@
             rows,
             rows,
             jax.ShapeDtypeStruct((GROUP, HD), jnp.float32),
+            PARTS,
+            jax.ShapeDtypeStruct((2, GROUP, HD), jnp.float32),
         ),
         in_specs=[HBM] * 5,
-        out_specs=(HBM,) * 6,
+        out_specs=(HBM,) * 8,
         scratch_shapes=[
             pltpu.VMEM(WHOLE, jnp.bfloat16),
             pltpu.VMEM(WHOLE, jnp.bfloat16),
             pltpu.VMEM((NS, 2, SB, BR, HD), jnp.bfloat16),
+            pltpu.VMEM((NS, SB, BR, HD), jnp.bfloat16),
+            pltpu.VMEM((2, GROUP, HD), jnp.float32),
             pltpu.VMEM(PACKED, jnp.bfloat16),
             pltpu.VMEM(PACKED, jnp.bfloat16),
             pltpu.VMEM(ROWS, jnp.float32),
@@ -505,6 +608,8 @@
             dma((NZ,)),
             dma((NZ,)),
             dma((NZ + 1, NC)),
+            dma,
+            dma,
         ],
         compiler_params=pltpu.CompilerParams(
             collective_id=0, has_side_effects=True, vmem_limit_bytes=VMEM_BYTES
@@ -513,17 +618,12 @@
     )(q, k, v, g, counts)
 
 
-def return_kernel(count, *refs):
-    ins, outs = refs[:count], refs[count : 2 * count]
-    loc, ssem, rsem = refs[2 * count :]
+def return_kernel(grads, out, loc, ssem, rsem):
     z, x, core, tp = place()
     here = x * NC + core
     partners = [(dx, dc) for dx in (2, 1, 3, 0) for dc in range(NC) if dx + dc > 0]
-    own = []
-    for a in range(count):
-        cp = pltpu.make_async_copy(ins[a].at[here], outs[a].at[x, :, lax.rem(core + here, NC)], loc.at[a])
-        cp.start()
-        own.append(cp)
+    own = pltpu.make_async_copy(grads.at[here], out.at[x, :, :, lax.rem(core + here, NC)], loc)
+    own.start()
     barrier = pltpu.get_barrier_semaphore()
     for dx, dc in partners:
         dev = (ctx_of(z, lax.rem(x + dx, NX), lax.rem(core + dc, NC)), tp)
@@ -533,77 +633,73 @@
     for dx, dc in partners:
         px, pc = lax.rem(x + dx, NX), lax.rem(core + dc, NC)
         there = px * NC + pc
-        for a in range(count):
-            cp = remote(
-                ins[a].at[there],
-                outs[a].at[x, :, lax.rem(core + there, NC)],
-                ssem.at[a, dx, dc],
-                rsem.at[a, dx, dc],
-                (ctx_of(z, px, pc), tp),
-            )
-            cp.start()
-            sends.append(cp)
-    for cp in own:
-        cp.wait()
+        cp = remote(
+            grads.at[there],
+            out.at[x, :, :, lax.rem(core + there, NC)],
+            ssem.at[dx, dc],
+            rsem.at[dx, dc],
+            (ctx_of(z, px, pc), tp),
+        )
+        cp.start()
+        sends.append(cp)
+    own.wait()
     for dx, dc in partners:
         ox, oc = lax.rem(x + NX - dx, NX), lax.rem(core + NC - dc, NC)
-        for a in range(count):
-            ref = outs[a].at[ox, :, lax.rem(oc + here, NC)]
-            remote(
-                ins[a].at[here], ref, ssem.at[a, dx, dc], rsem.at[a, dx, dc], (ctx_of(z, ox, oc), tp)
-            ).wait_recv()
+        ref = out.at[ox, :, :, lax.rem(oc + here, NC)]
+        remote(grads.at[here], ref, ssem.at[dx, dc], rsem.at[dx, dc], (ctx_of(z, ox, oc), tp)).wait_recv()
     for cp in sends:
         cp.wait_send()
 
 
-def return_heads(*arrays):
-    count = len(arrays)
+def return_heads(grads):
     dma = pltpu.SemaphoreType.DMA
     return pl.pallas_call(
-        functools.partial(return_kernel, count),
-        out_shape=(LANDED,) * count,
-        in_specs=[HBM] * count,
-        out_specs=(HBM,) * count,
-        scratch_shapes=[dma((count,)), dma((count, NX, NC)), dma((count, NX, NC))],
+        return_kernel,
+        out_shape=LANDED3,
+        in_specs=[HBM],
+        out_specs=HBM,
+        scratch_shapes=[dma, dma((NX, NC)), dma((NX, NC))],
         compiler_params=pltpu.CompilerParams(collective_id=1, has_side_effects=True),
         name="return_heads",
-    )(*arrays)
-
-
-def assemble_kernel(count, *refs):
-    ins, outs = refs[:count], refs[count : 2 * count]
-    bufs, res, lsem, ssem = refs[2 * count : 2 * count + 4]
-    loads = [pltpu.make_async_copy(ins[a], bufs.at[a], lsem.at[a]) for a in range(count)]
-    stores = [pltpu.make_async_copy(res.at[a], outs[a], ssem.at[a]) for a in range(count)]
+    )(grads)
+
+
+def assemble_kernel(att, grads, *refs):
+    outs = refs[:4]
+    buf0, buf, res, lsem, ssem = refs[4:]
+    loads = [pltpu.make_async_copy(att, buf0, lsem.at[0])]
+    loads += [pltpu.make_async_copy(grads.at[:, a], buf.at[:, a], lsem.at[a + 1]) for a in range(3)]
     for cp in loads:
         cp.start()
-    for a in range(count):
+    stores = [pltpu.make_async_copy(res.at[a], outs[a], ssem.at[a]) for a in range(4)]
+    for a in range(4):
         loads[a].wait()
         for i in range(NX):
-            res[a, :, i * HD : (i + 1) * HD] = bufs[a, i].reshape(CAP, HD)
+            part = buf0[i] if a == 0 else buf[i, a - 1]
+            res[a, :, i * HD : (i + 1) * HD] = part.reshape(CAP, HD)
         stores[a].start()
     for cp in stores:
         cp.wait()
 
 
-def assemble(*arrays):
-    count = len(arrays)
+def assemble(att, grads):
     dma = pltpu.SemaphoreType.DMA
     shape = jax.ShapeDtypeStruct((CAP, NX * HD), jnp.bfloat16)
     return pl.pallas_call(
-        functools.partial(assemble_kernel, count),
-        out_shape=(shape,) * count,
-        in_specs=[HBM] * count,
-        out_specs=(HBM,) * count,
+        assemble_kernel,
+        out_shape=(shape,) * 4,
+        in_specs=[HBM] * 2,
+        out_specs=(HBM,) * 4,
         scratch_shapes=[
-            pltpu.VMEM((count,) + LANDED.shape, jnp.bfloat16),
-            pltpu.VMEM((count, CAP, NX * HD), jnp.bfloat16),
-            dma((count,)),
-            dma((count,)),
+            pltpu.VMEM(LANDED.shape, jnp.bfloat16),
+            pltpu.VMEM(LANDED3.shape, jnp.bfloat16),
+            pltpu.VMEM((4, CAP, NX * HD), jnp.bfloat16),
+            dma((4,)),
+            dma((4,)),
         ],
         compiler_params=pltpu.CompilerParams(vmem_limit_bytes=VMEM_BYTES),
         name="assemble",
-    )(*arrays)
+    )(att, grads)
 
 
 def fill_offsets(counts, off, z, sign, planes):
@@ -659,8 +755,8 @@
 
 
 def backward_kernel(
-    counts_hbm, qg, kv, st, info, stcol, dq_out, dk_out, dv_out,
-    counts, koff, qoff, kvc, qgc, stv, infov, qrow, krow, col, dqa, dka, dva, res,
+    counts_hbm, qg, kv, st, info, stcol, dq_in, dkv_in, grads,
+    counts, koff, qoff, kvc, qgc, stv, infov, qrow, krow, col, dqa, dka, dva, res, dkv, begin,
     csem, ksem, qsem, ssem, osem,
 ):
     z, x, core, _ = place()
@@ -673,14 +769,37 @@
     for small in smalls:
         small.start()
     cp.wait()
-    kplanes, qplanes = z + 1, NZ - z
+    top = z == NZ - 1
+    early = pltpu.make_async_copy(dq_in, res.at[:, 0], osem.at[0])
+
+    @pl.when(z < NZ - 1)
+    def _():
+        early.start()
+
+    dkv_copy = pltpu.make_async_copy(dkv_in, dkv, osem.at[2])
+
+    @pl.when(z == 0)
+    def _():
+        dkv_copy.start()
+
+    @pl.when(z > 0)
+    def _():
+        def clear(j, _):
+            for part in range(2):
+                dkv[part, pl.ds(pl.multiple_of(j * SEG, SEG), SEG), :] = jnp.zeros((SEG, HD), jnp.float32)
+            return 0
+
+        lax.fori_loop(0, NS, clear, 0)
+
+    zq = jnp.where(z == 0, NZ - 1, z)
+    kplanes, qplanes = jnp.where(top, NZ, 1), NZ - zq
     fill_offsets(counts, koff, z, -1, kplanes)
     load(koff, kv, kvc, ksem, z, -1, kplanes, False)
-    fill_offsets(counts, qoff, z, 1, qplanes)
-    load(qoff, qg, qgc, qsem, z, 1, qplanes, False)
+    fill_offsets(counts, qoff, zq, 1, qplanes)
+    load(qoff, qg, qgc, qsem, zq, 1, qplanes, False)
     key_end = koff[kplanes * NC]
     query_end = qoff[qplanes * NC]
-    plane_end = koff[NC]
+    plane_end = jnp.where(z == 0, 0, koff[NC])
     zero = jnp.zeros((GROUP // BR, BR, HD), jnp.bfloat16)
     for part in range(2):
         kvc[part, pl.ds(key_end, GROUP // BR)] = zero
@@ -688,14 +807,15 @@
     for small in smalls:
         small.wait()
     line_up(koff, infov, krow, z, -1, kplanes, -FAR)
-    line_up(qoff, stv, qrow, z, 1, qplanes, FAR)
+    line_up(qoff, stv, qrow, zq, 1, qplanes, FAR)
     base = koff[core]
     total = koff[core + 1] - base
     starts = [jnp.int32(0)]
     for j in range(NS):
         starts.append(starts[-1] + live_blocks(counts, z, core, j))
+        begin[j] = starts[j]
     load(koff, kv, kvc, ksem, z, -1, kplanes, True)
-    load(qoff, qg, qgc, qsem, z, 1, qplanes, True)
+    load(qoff, qg, qgc, qsem, zq, 1, qplanes, True)
 
     def tile(buf, part, t):
         return buf[part, pl.ds(t * (T // BR), T // BR)].reshape(T, HD)
@@ -741,7 +861,7 @@
 
         per = T // BR
         lax.fori_loop(0, (query_end + per - 1) // per, key_step, 0)
-        lax.fori_loop(0, (key_end + per - 1) // per, query_step, 0)
+        lax.fori_loop(0, jnp.where(top, (key_end + per - 1) // per, 0), query_step, 0)
 
     lower = 0
     for size in SIZES:
@@ -753,29 +873,47 @@
         lower = size
 
     r = lax.broadcasted_iota(jnp.int32, (SEG, HD), 0)
-    stores = []
-    for a, (src, dst, scale) in enumerate(((dka, dk_out, SCALE), (dva, dv_out, 1.0), (dqa, dq_out, SCALE))):
-        for j in range(NS):
+
+    def spread(a, src, scale, more):
+        def step(j, _):
             row = r + (r // BR + lax.rem(core + j, NC)) * BR
-            part = src[pl.ds(pl.multiple_of(starts[j] * BR, BR), SEG), :] * scale
-            part = jnp.where(row < counts[z * NS + j], part, 0.0)
-            res[a, j] = part.astype(jnp.bfloat16).reshape(SB, BR, HD)
-        cp = pltpu.make_async_copy(res.at[a], dst, osem.at[a])
-        cp.start()
-        stores.append(cp)
-    for cp in stores:
-        cp.wait()
-
-
-def backward(counts, qg, kv, st, info, stcol):
+            part = src[pl.ds(pl.multiple_of(begin[j] * BR, BR), SEG), :]
+            if more is not None:
+                part = part + dkv[more, pl.ds(pl.multiple_of(j * SEG, SEG), SEG), :]
+            part = jnp.where(row < counts[z * NS + j], part * scale, 0.0)
+            res[j, a] = part.astype(jnp.bfloat16).reshape(SB, BR, HD)
+            return 0
+
+        lax.fori_loop(0, NS, step, 0)
+
+    @pl.when(z == 0)
+    def _():
+        dkv_copy.wait()
+
+    spread(1, dka, SCALE, 0)
+    spread(2, dva, 1.0, 1)
+
+    @pl.when(top)
+    def _():
+        spread(0, dqa, SCALE, None)
+
+    @pl.when(z < NZ - 1)
+    def _():
+        early.wait()
+
+    store = pltpu.make_async_copy(res, grads, osem.at[1])
+    store.start()
+    store.wait()
+
+
+def backward(counts, qg, kv, st, info, stcol, dq, dkv):
     dma = pltpu.SemaphoreType.DMA
-    parts = jax.ShapeDtypeStruct((NS, SB, BR, HD), jnp.bfloat16)
     blocks = (KEYS + GROUP + T) // BR
     return pl.pallas_call(
         backward_kernel,
-        out_shape=(parts, parts, parts),
-        in_specs=[HBM] * 6,
-        out_specs=(HBM,) * 3,
+        out_shape=GRADS,
+        in_specs=[HBM] * 8,
+        out_specs=HBM,
         scratch_shapes=[
             pltpu.SMEM((NZ * NS,), jnp.int32),
             pltpu.SMEM((NZ * NC + 1,), jnp.int32),
@@ -790,7 +928,9 @@
             pltpu.VMEM((GROUP + SEG, HD), jnp.float32),
             pltpu.VMEM((GROUP + SEG, HD), jnp.float32),
             pltpu.VMEM((GROUP + SEG, HD), jnp.float32),
-            pltpu.VMEM((3, NS, SB, BR, HD), jnp.bfloat16),
+            pltpu.VMEM(GRADS.shape, jnp.bfloat16),
+            pltpu.VMEM((2, GROUP, HD), jnp.float32),
+            pltpu.SMEM((NS,), jnp.int32),
             dma,
             dma((NZ * NC,)),
             dma((NZ * NC,)),
@@ -799,18 +939,18 @@
         ],
         compiler_params=pltpu.CompilerParams(vmem_limit_bytes=VMEM_BYTES),
         name="backward",
-    )(counts, qg, kv, st, info, stcol)
+    )(counts, qg, kv, st, info, stcol, dq, dkv)
 
 
 def on_device(query_heads, key_heads, value_heads, grad_heads, counts):
     def blocks(array):
         return array.reshape(SB, 2, BR, NX * HD)
 
-    kv, qg, att, st, info, stcol = attend(
+    kv, qg, att, st, info, stcol, dq, dkv = attend(
         blocks(query_heads), blocks(key_heads), blocks(value_heads), blocks(grad_heads), counts
     )
-    dq, dk, dv = backward(counts, qg, kv, st, info, stcol)
-    return assemble(att, *return_heads(dq, dk, dv))
+    grads = backward(counts, qg, kv, st, info, stcol, dq, dkv)
+    return tuple(assemble(att, return_heads(grads)))
 
 
 def solution(mesh):

time: 92 us -> 89.6 us (0.974)
  the two profiles are of different devices: /device:TPU:33 before, /device:TPU:241 now
where the time goes in v2:
time: 89.6 us; the launch traced here: 89.5 us
  Pallas kernels  88.7 us (99%)
    pallas_call x1, Pallas kernels, attend(): pl.pallas_call(attend_kernel, out_shape=(packed, packed, LANDED, rows, ro...  55.4 us
    pallas_call x1, Pallas kernels, backward(): pl.pallas_call(backward_kernel, out_shape=GRADS, in_specs=[HBM] * 8, out_...  18.3 us
    pallas_call x1, Pallas kernels, return_heads(): pl.pallas_call(return_kernel, out_shape=LANDED3, in_specs=[HBM], out_spec...  13 us
    pallas_call x1, Pallas kernels, assemble(): pl.pallas_call(assemble_kernel, out_shape=(shape,) * 4, in_specs=[HBM] *...  2.03 us

profile of v2, /device:TPU:241, one launch (start us, length us, event | category | flops | bytes accessed | tf_op | source)
XLA Modules:
  0.0 89.5 jit_solution(9994774331595990820)
XLA Ops:
  0.6 55.4 %attend.1 = (bf16[4,2,2,64,16,128]{5,4,3,2,1,0:T(8,128)(2,1)}, bf16[4,2,2,64,16,128]{5,4,3,2,1,0:T(8,128)(2,1)}, bf16[4,8,2,16,128]{4,3,2,1,0:T(8,128)(2,1)}, f3...) custom-call(bf16[8,2,16,512]{3,2,1,0:T(8,128)(2,1)} %bitcast.4, ...), custom_call_target="tpu_custom_call" | custom-call | tf_op jit(solution)/shard_map/attend/pallas_call | solution.py:560
  56.0 18.3 %backward.1.grads = bf16[8,3,8,16,128]{4,3,2,1,0:T(8,128)(2,1)} custom-call(s32[32]{0:T(128)} %counts_hbm.3, bf16[4,2,2,64,16,128]{5,4,3,2,1,0:T(8,128)(2,1)} %get-tuple-element.13.qg, bf16[4,2,2,64,16,128]{5,4,3,2,1,0:T(8,128)(2,1)} %get-tuple-element.14.kv, f32[4,2,8,1024]{3,2,1,0:T(8,128)} %get-tuple-element.15.st, ...), custom_call_target="tpu_custom_call" | custom-call | tf_op jit(solution)/shard_map/backward/pallas_call | solution.py:912
  74.3 13.0 %return_heads.1.grads = bf16[4,3,8,2,16,128]{5,4,3,2,1,0:T(8,128)(2,1)} custom-call(bf16[8,3,8,16,128]{4,3,2,1,0:T(8,128)(2,1)} %backward.1.grads), custom_call_target="tpu_custom_call" | custom-call | tf_op jit(solution)/shard_map/return_heads/pallas_call | solution.py:656
  87.3 2.0 %assemble.1 = (bf16[256,512]{1,0:T(8,128)(2,1)}, bf16[256,512]{1,0:T(8,128)(2,1)}, bf16[256,512]{1,0:T(8,128)(2,1)}, bf16[256,512]{1,0:T(8,128)(2,1)}) custom-call(bf16[4,8,2,16,128]{4,3,2,1,0:T(8,128)(2,1)} %get-tuple-element.12.att, bf16[4,3,8,2,16,128]{5,4,3,2,1,0:T(8,128)(2,1)} %return_heads.1.grads), custom_call_target="tpu_custom_call" | custom-call | tf_op jit(solution)/shard_map/assemble/pallas_call | solution.py:688

commit v3 on v2

--- a/solution.py
+++ b/solution.py
@@ -228,14 +228,14 @@
                 inside = (2 * (line // BR) + (c + jj) % 2) * BR + lax.rem(line, BR)
                 queries.append((p * NS + 2 * xs + jj) * CAP + inside)
         for j in range(NS):
-            keys.append(j * CAP + (2 * (inner // BR) + lax.rem(core + j, NC)) * BR + lax.rem(inner, BR))
+            keys.append((z * NS + j) * CAP + (2 * (inner // BR) + lax.rem(core + j, NC)) * BR + lax.rem(inner, BR))
         qq, gg = jnp.concatenate(qs, axis=0), jnp.concatenate(gs, axis=0)
         lse, delta = jnp.concatenate(lses, axis=1), jnp.concatenate(deltas, axis=1)
-        s = dot(kvs[0, core, :, 0].reshape(GROUP, HD), qq, NT) * SCALE2
+        s = dot(kvs[z, core, :, 0].reshape(GROUP, HD), qq, NT) * SCALE2
         pr = jnp.exp2(s - lse)
         pr = jnp.where(jnp.concatenate(keys, axis=0) <= jnp.concatenate(queries, axis=1), pr, 0.0)
         dkv[1] += dot(pr.astype(jnp.bfloat16), gg, NN)
-        dp = dot(kvs[0, core, :, 1].reshape(GROUP, HD), gg, NT)
+        dp = dot(kvs[z, core, :, 1].reshape(GROUP, HD), gg, NT)
         dkv[0] += dot((pr * (dp - delta)).astype(jnp.bfloat16), qq, NN)
 
     flows = ((kvs, -1, has_up, above), (qgs, 1, has_dn, below))
@@ -315,7 +315,7 @@
         def _():
             pack(kvs, kvp, z - d)
 
-        @pl.when(whole & (z > 0) & (z + d < NZ))
+        @pl.when(whole & (z + d < NZ) & ((z > 1) | (z + d == NZ - 1)))
         def _():
             pack(qgs, qgp, z + d)
 
@@ -385,7 +385,7 @@
 
     top = z == NZ - 1
     done = jnp.where(z == 0, 1, 4 * z)
-    pace = jnp.where(z == NZ - 2, 3, 1)
+    pace = jnp.where(z == NZ - 2, 3, jnp.where(z == 1, 2, 1))
 
     def back(u, _):
         d, m, xs = place_of(u)
@@ -393,10 +393,11 @@
         return 0
 
     def key_work(w, _):
-        p, m, xs = place_of(w)
+        d, m, xs = place_of(w)
+        p = z + d
         for c in range(NC):
 
-            @pl.when((m == 0) & ((p > 0) | (c != core)))
+            @pl.when((m == 0) & ((d > 0) | (c != core)))
             def _():
                 ref = stv.at[p, c]
                 remote(ref, ref, sst.at[0], rst.at[p, c], sib).wait_recv()
@@ -418,12 +419,14 @@
         @pl.when((t > done) & (z < NZ - 1))
         def _():
             first = (t - done - 1) * pace
-            last = jnp.minimum(first + pace, NX * (z + 1))
+            last = jnp.maximum(first, jnp.minimum(first + pace, NX * (z + 1)))
             lax.fori_loop(first, last, back, 0)
 
-        @pl.when((z == 0) & (t >= 6) & (t < 12))
+        start = jnp.where(z == 0, 6, 9)
+
+        @pl.when((z <= 1) & (t >= start) & (t < start + 2 * (NZ - 1 - z)))
         def _():
-            lax.fori_loop(2 * t - 12, 2 * t - 10, key_work, 0)
+            lax.fori_loop(2 * (t - start), 2 * (t - start) + 2, key_work, 0)
 
         return 0
 
@@ -437,7 +440,7 @@
             dqs[j] = (acc[:, rows] * SCALE).T.astype(jnp.bfloat16).reshape(SB, BR, HD)
         pltpu.make_async_copy(dqs, dq_out, sdq).start()
 
-    @pl.when(z == 0)
+    @pl.when(z <= 1)
     def _():
         pltpu.make_async_copy(dkv, dkv_out, sdkv).start()
 
@@ -464,18 +467,18 @@
             def _():
                 act(pltpu.make_async_copy(kvp.at[z - dz], kv_out.at[z - dz], okv.at[z - dz]))
 
-            @pl.when((z + dz < NZ) & ((z > 0) | (dz == NZ - 1)))
+            @pl.when((z + dz < NZ) & ((z > 1) | (z + dz == NZ - 1)))
             def _():
                 act(pltpu.make_async_copy(qgp.at[z + dz], qg_out.at[z + dz], oqg.at[z + dz]))
 
-        @pl.when(z > 0)
+        @pl.when(z > 1)
         def _():
             act(pltpu.make_async_copy(stats, st_out.at[z, core], ost.at[z, core]))
             take(z, 1 - core)
 
         for dz in range(1, NZ):
 
-            @pl.when((z + dz < NZ) & ((z > 0) | (dz == NZ - 1)))
+            @pl.when((z + dz < NZ) & ((z > 1) | (z + dz == NZ - 1)))
             def _():
                 for c in range(NC):
                     take(z + dz, c)
@@ -504,7 +507,7 @@
     def _():
         pltpu.make_async_copy(dqs, dq_out, sdq).wait()
 
-    @pl.when(z == 0)
+    @pl.when(z <= 1)
     def _():
         pltpu.make_async_copy(dkv, dkv_out, sdkv).wait()
 
@@ -778,11 +781,11 @@
 
     dkv_copy = pltpu.make_async_copy(dkv_in, dkv, osem.at[2])
 
-    @pl.when(z == 0)
+    @pl.when(z <= 1)
     def _():
         dkv_copy.start()
 
-    @pl.when(z > 0)
+    @pl.when(z > 1)
     def _():
         def clear(j, _):
             for part in range(2):
@@ -791,7 +794,7 @@
 
         lax.fori_loop(0, NS, clear, 0)
 
-    zq = jnp.where(z == 0, NZ - 1, z)
+    zq = jnp.where(z <= 1, NZ - 1, z)
     kplanes, qplanes = jnp.where(top, NZ, 1), NZ - zq
     fill_offsets(counts, koff, z, -1, kplanes)
     load(koff, kv, kvc, ksem, z, -1, kplanes, False)
@@ -799,7 +802,7 @@
     load(qoff, qg, qgc, qsem, zq, 1, qplanes, False)
     key_end = koff[kplanes * NC]
     query_end = qoff[qplanes * NC]
-    plane_end = jnp.where(z == 0, 0, koff[NC])
+    plane_end = jnp.where(z <= 1, 0, koff[NC])
     zero = jnp.zeros((GROUP // BR, BR, HD), jnp.bfloat16)
     for part in range(2):
         kvc[part, pl.ds(key_end, GROUP // BR)] = zero
@@ -886,7 +889,7 @@
 
         lax.fori_loop(0, NS, step, 0)
 
-    @pl.when(z == 0)
+    @pl.when(z <= 1)
     def _():
         dkv_copy.wait()
 

time: 89.6 us -> 89.6 us (level); the launches traced: 89.5 us -> 88.5 us
  Pallas kernels: 88.7 us -> 87.7 us
where the time goes in v3:
time: 89.6 us; the launch traced here: 88.5 us
  Pallas kernels  87.7 us (98%)
    pallas_call x1, Pallas kernels, attend(): pl.pallas_call(attend_kernel, out_shape=(packed, packed, LANDED, rows, ro...  55.3 us
    pallas_call x1, Pallas kernels, backward(): pl.pallas_call(backward_kernel, out_shape=GRADS, in_specs=[HBM] * 8, out_...  17.4 us
    pallas_call x1, Pallas kernels, return_heads(): pl.pallas_call(return_kernel, out_shape=LANDED3, in_specs=[HBM], out_spec...  13 us
    pallas_call x1, Pallas kernels, assemble(): pl.pallas_call(assemble_kernel, out_shape=(shape,) * 4, in_specs=[HBM] *...  2.03 us

profile of v3, /device:TPU:241, one launch (start us, length us, event | category | flops | bytes accessed | tf_op | source)
XLA Modules:
  0.0 88.5 jit_solution(13197529726293774463)
XLA Ops:
  0.6 55.3 %attend.1 = (bf16[4,2,2,64,16,128]{5,4,3,2,1,0:T(8,128)(2,1)}, bf16[4,2,2,64,16,128]{5,4,3,2,1,0:T(8,128)(2,1)}, bf16[4,8,2,16,128]{4,3,2,1,0:T(8,128)(2,1)}, f3...) custom-call(bf16[8,2,16,512]{3,2,1,0:T(8,128)(2,1)} %bitcast.4, ...), custom_call_target="tpu_custom_call" | custom-call | tf_op jit(solution)/shard_map/attend/pallas_call | solution.py:563
  56.0 17.4 %backward.1.grads = bf16[8,3,8,16,128]{4,3,2,1,0:T(8,128)(2,1)} custom-call(s32[32]{0:T(128)} %counts_hbm.3, bf16[4,2,2,64,16,128]{5,4,3,2,1,0:T(8,128)(2,1)} %get-tuple-element.13.qg, bf16[4,2,2,64,16,128]{5,4,3,2,1,0:T(8,128)(2,1)} %get-tuple-element.14.kv, f32[4,2,8,1024]{3,2,1,0:T(8,128)} %get-tuple-element.15.st, ...), custom_call_target="tpu_custom_call" | custom-call | tf_op jit(solution)/shard_map/backward/pallas_call | solution.py:915
  73.4 13.0 %return_heads.1.grads = bf16[4,3,8,2,16,128]{5,4,3,2,1,0:T(8,128)(2,1)} custom-call(bf16[8,3,8,16,128]{4,3,2,1,0:T(8,128)(2,1)} %backward.1.grads), custom_call_target="tpu_custom_call" | custom-call | tf_op jit(solution)/shard_map/return_heads/pallas_call | solution.py:659
  86.3 2.0 %assemble.1 = (bf16[256,512]{1,0:T(8,128)(2,1)}, bf16[256,512]{1,0:T(8,128)(2,1)}, bf16[256,512]{1,0:T(8,128)(2,1)}, bf16[256,512]{1,0:T(8,128)(2,1)}) custom-call(bf16[4,8,2,16,128]{4,3,2,1,0:T(8,128)(2,1)} %get-tuple-element.12.att, bf16[4,3,8,2,16,128]{5,4,3,2,1,0:T(8,128)(2,1)} %return_heads.1.grads), custom_call_target="tpu_custom_call" | custom-call | tf_op jit(solution)/shard_map/assemble/pallas_call | solution.py:691

commit v4 on v3

--- a/solution.py
+++ b/solution.py
@@ -384,7 +384,7 @@
         stay.start()
 
     top = z == NZ - 1
-    done = jnp.where(z == 0, 1, 4 * z)
+    done = jnp.where(z == 0, 1, 4 * z - 1)
     pace = jnp.where(z == NZ - 2, 3, jnp.where(z == 1, 2, 1))
 
     def back(u, _):
@@ -410,7 +410,7 @@
         def _():
             comm(t)
 
-        lax.fori_loop(jnp.where(t < 3, 2 * t, t + 3), jnp.where(t < 3, 2 * t + 2, t + 4), work, 0)
+        lax.fori_loop(jnp.where(t < 4, 2 * t, t + 4), jnp.where(t < 4, 2 * t + 2, t + 5), work, 0)
 
         @pl.when(t == done)
         def _():
@@ -422,7 +422,7 @@
             last = jnp.maximum(first, jnp.minimum(first + pace, NX * (z + 1)))
             lax.fori_loop(first, last, back, 0)
 
-        start = jnp.where(z == 0, 6, 9)
+        start = jnp.where(z == 0, 6, 8)
 
         @pl.when((z <= 1) & (t >= start) & (t < start + 2 * (NZ - 1 - z)))
         def _():
@@ -431,7 +431,7 @@
         return 0
 
     lax.fori_loop(0, NX, own_step, 0)
-    lax.fori_loop(0, (NZ - 1) * NX + 1, step, 0)
+    lax.fori_loop(0, (NZ - 1) * NX, step, 0)
 
     @pl.when(z < NZ - 1)
     def _():

time: 89.6 us -> 90.7 us (1.012)
  Pallas kernels: 87.7 us -> 88.8 us
    pallas_call x1, Pallas kernels: 55.3 us -> 59 us  [attend(): pl.pallas_call(attend_kernel, out_shape=(packed, packed, LANDED, rows, ro...]
    pallas_call x1, Pallas kernels: 17.4 us -> 14.8 us  [backward(): pl.pallas_call(backward_kernel, out_shape=GRADS, in_specs=[HBM] * 8, out_...]
where the time goes in v4:
time: 90.7 us; the launch traced here: 89.6 us
  Pallas kernels  88.8 us (98%)
    pallas_call x1, Pallas kernels, attend(): pl.pallas_call(attend_kernel, out_shape=(packed, packed, LANDED, rows, ro...  59 us
    pallas_call x1, Pallas kernels, backward(): pl.pallas_call(backward_kernel, out_shape=GRADS, in_specs=[HBM] * 8, out_...  14.8 us
    pallas_call x1, Pallas kernels, return_heads(): pl.pallas_call(return_kernel, out_shape=LANDED3, in_specs=[HBM], out_spec...  13 us
    pallas_call x1, Pallas kernels, assemble(): pl.pallas_call(assemble_kernel, out_shape=(shape,) * 4, in_specs=[HBM] *...  2.03 us

profile of v4, /device:TPU:241, one launch (start us, length us, event | category | flops | bytes accessed | tf_op | source)
XLA Modules:
  0.0 89.6 jit_solution(8985885247397931394)
XLA Ops:
  0.6 59.0 %attend.1 = (bf16[4,2,2,64,16,128]{5,4,3,2,1,0:T(8,128)(2,1)}, bf16[4,2,2,64,16,128]{5,4,3,2,1,0:T(8,128)(2,1)}, bf16[4,8,2,16,128]{4,3,2,1,0:T(8,128)(2,1)}, f3...) custom-call(bf16[8,2,16,512]{3,2,1,0:T(8,128)(2,1)} %bitcast.4, ...), custom_call_target="tpu_custom_call" | custom-call | tf_op jit(solution)/shard_map/attend/pallas_call | solution.py:563
  59.6 14.8 %backward.1.grads = bf16[8,3,8,16,128]{4,3,2,1,0:T(8,128)(2,1)} custom-call(s32[32]{0:T(128)} %counts_hbm.3, bf16[4,2,2,64,16,128]{5,4,3,2,1,0:T(8,128)(2,1)} %get-tuple-element.13.qg, bf16[4,2,2,64,16,128]{5,4,3,2,1,0:T(8,128)(2,1)} %get-tuple-element.14.kv, f32[4,2,8,1024]{3,2,1,0:T(8,128)} %get-tuple-element.15.st, ...), custom_call_target="tpu_custom_call" | custom-call | tf_op jit(solution)/shard_map/backward/pallas_call | solution.py:915
  74.4 13.0 %return_heads.1.grads = bf16[4,3,8,2,16,128]{5,4,3,2,1,0:T(8,128)(2,1)} custom-call(bf16[8,3,8,16,128]{4,3,2,1,0:T(8,128)(2,1)} %backward.1.grads), custom_call_target="tpu_custom_call" | custom-call | tf_op jit(solution)/shard_map/return_heads/pallas_call | solution.py:659
  87.4 2.0 %assemble.1 = (bf16[256,512]{1,0:T(8,128)(2,1)}, bf16[256,512]{1,0:T(8,128)(2,1)}, bf16[256,512]{1,0:T(8,128)(2,1)}, bf16[256,512]{1,0:T(8,128)(2,1)}) custom-call(bf16[4,8,2,16,128]{4,3,2,1,0:T(8,128)(2,1)} %get-tuple-element.12.att, bf16[4,3,8,2,16,128]{5,4,3,2,1,0:T(8,128)(2,1)} %return_heads.1.grads), custom_call_target="tpu_custom_call" | custom-call | tf_op jit(solution)/shard_map/assemble/pallas_call | solution.py:691
